TPU v7x, 256 devices: a whole 4x4x8 slice. The times are simulated.
256 devices in a mesh: ex: 32 (over z, y_lo, core), feat: 8 (over y_hi, x).
Axes of the slice: x: 4, y: 4 (y_hi: 2, y_lo: 2; y = y_hi * 2 + y_lo), z: 8, core: 2. Of those that a mesh axis runs over, the one named last changes fastest.
Arguments:
- grads: bfloat16 [8192, 8192], P('ex', 'feat'), may hold values from -6 to 6
- lr_plan: float32 [64], replicated, may hold values from 0.1 to 1
- ckpt_step: int32 [4], replicated, may hold values from 0 to 63
Outputs:
- influence: float32 [8192, 8192], P('ex', 'feat')
All inputs are finite; a program needn't handle non-finite values.
Results may differ from a plain program's by a relative error of at most 0.003.
Values may be sent and summed in bfloat16 or wider, within the bound.
No kernel may reach another device: no remote copies, remote signals or barrier semaphores. Data moves between devices by JAX's collectives and lax.ppermute only.
A program may use at most 64 MiB of HBM per device.

v0:
```python
import jax
import jax.numpy as jnp
from jax import lax
from jax.sharding import PartitionSpec as P

PROJ = 2048
CKPT = 4
FEATURES = 8192


def pair_block(rows_left, rows_right):
    return lax.dot_general(
        rows_left, rows_right, (((1,), (1,)), ((), ())), preferred_element_type=jnp.float32
    )


def on_device(grads, lr_plan, ckpt_step):
    sched_ids = jnp.arange(lr_plan.shape[0], dtype=jnp.int32)
    rate = jnp.sum(
        jnp.where(ckpt_step[:, None] == sched_ids[None, :], lr_plan[None, :], 0.0), axis=1
    )
    weight = rate / jnp.sum(rate) * (CKPT / jnp.sqrt(jnp.float32(FEATURES)))
    width = grads.shape[1]
    columns = lax.axis_index("feat") * width + jnp.arange(width, dtype=jnp.int32)
    owner = columns // PROJ
    ckpt_ids = jnp.arange(CKPT, dtype=jnp.int32)
    column_weight = jnp.sum(
        jnp.where(owner[:, None] == ckpt_ids[None, :], weight[None, :], 0.0), axis=1
    )
    scaled = (grads.astype(jnp.float32) * jnp.sqrt(column_weight)[None, :]).astype(jnp.bfloat16)
    partial_rows = pair_block(scaled, lax.all_gather(scaled, "ex", axis=0, tiled=True))
    result = lax.psum_scatter(partial_rows, "feat", scatter_dimension=1, tiled=True)
    return result


def solution(mesh):
    in_specs = (P("ex", "feat"), P(), P())
    out_specs = P("ex", "feat")
    return jax.shard_map(
        on_device, mesh=mesh, in_specs=in_specs, out_specs=out_specs, check_vma=False
    )
```

profile of v0, /device:TPU:1, one launch (start us, length us, event | category | flops | bytes accessed | tf_op | source)
XLA Modules:
  0.0 255.0 jit_solution(16870369013536467004)
XLA Ops:
  6.5 0.0 all-gather.2.cloned.1.call-start
  6.5 1.4 select_reduce_fusion.1
  7.9 0.6 divide_multiply_fusion
  8.6 0.1 select_reduce_fusion
  8.7 1.9 multiply_convert_fusion
  10.6 0.0 all-gather.2.cloned.1.call-update
  10.7 0.0 reduce-scatter.2.cloned.1.call-start
  10.7 104.1 %all-gather.2.cloned.1.call-done = bf16[8192,1024]{1,0:T(8,128)(2,1)} async-done(((bf16[256,1024]{1,0:T(8,128)(2,1)}), bf16[8192,1024]{1,0:T(8,128)(2,1)}) %all-gather.2.cloned.1.call-update) | async-done | bytes 16777232 | tf_op jit(solution)/shard_map/all_gather | solution.py:31
  114.8 13.7 %fusion.3 = f32[256,8192]{1,0:T(8,128)} fusion(bf16[256,1024]{1,0:T(8,128)(2,1)} %multiply_convert_fusion, bf16[8192,1024]{1,0:T(8,128)(2,1)} %all-gather.2.cloned.1.call-done), kind=kOutput, calls=%fused_computation.16 | convolution fusion | flops 4294967296 | bytes 25690112 | tf_op jit(solution)/shard_map/dot_general | solution.py:12
  128.5 0.0 reduce-scatter.2.cloned.1.call-update
  128.5 119.6 %reduce-scatter.2.cloned.1.call-done = f32[256,1024]{1,0:T(8,128)} async-done(((f32[256,8192]{1,0:T(8,128)}), f32[256,1024]{1,0:T(8,128)}) %reduce-scatter.2.cloned.1.call-update) | async-done | bytes 1048592 | tf_op jit(solution)/shard_map/reduce_scatter | solution.py:32
  (2 shorter events, 0.0 us)
Async XLA Ops:
  6.5 108.3 %all-gather.2.cloned.1.call-start = ((), (), s32[]{:S(2)}) async-start(), calls=%async_computation.1 | async-start | bytes 17301504 | tf_op jit(solution)/shard_map/all_gather | solution.py:31
  10.7 237.5 %reduce-scatter.2.cloned.1.call-start = ((), (), s32[]{:S(2)}) async-start(), calls=%async_computation.2 | async-start | bytes 9437184 | tf_op jit(solution)/shard_map/reduce_scatter | solution.py:32
Sparse Core Ops, SparseCore 0:
  10.8 103.9 all-gather.1
  128.7 119.4 reduce-scatter.1
where the time goes:
time: 255 us
  waiting for transfers between devices  224 us (88%)
  matrix products  13.7 us (5%)
  between operations  13.4 us (5%)
  other arithmetic  4.08 us (2%)
    reduce_scatter x1, waiting for transfers between devices, on_device(): lax.psum_scatter(partial_rows, 'feat', scatter_dimension=1, tiled=True)  120 us
    all_gather x1, waiting for transfers between devices, on_device(): lax.all_gather(scaled, 'ex', axis=0, tiled=True)  104 us
    dot_general x1, matrix products, pair_block(): lax.dot_general(rows_left, rows_right, (((1,), (1,)), ((), ())), preferre...  13.7 us
  transfers between devices with their start and end apart: 2, of which 2 were waited for; matrix products, arithmetic and copies ran while one was open for 0% of the time, Pallas kernels for 0%

commit v1 on v0

v1 whole, which is shorter than its diff:
```python
import jax
import jax.numpy as jnp
from jax import lax
from jax.experimental import pallas as pl
from jax.experimental.pallas import tpu as pltpu
from jax.sharding import Mesh, PartitionSpec as P

PROJ = 2048
CKPT = 4
FEATURES = 8192

Z, YL, C, YH, X = "z", "ylo", "core", "yhi", "x"
NZ, NX = 8, 4
SMEM = pl.BlockSpec(memory_space=pltpu.SMEM)
VMEM = pl.BlockSpec(memory_space=pltpu.VMEM)
HBM = pl.BlockSpec(memory_space=pltpu.HBM)


def take_from(value, axis, size, step):
    return lax.ppermute(value, axis, [(i, (i - step) % size) for i in range(size)])


def dot_t(left, right):
    return lax.dot_general(left, right, (((1,), (1,)), ((), ())), preferred_element_type=jnp.float32)


def scale_kernel(plan_ref, step_ref, grads_ref, out_ref, *quarter_refs):
    x = lax.axis_index(X)
    mine = ((lax.axis_index(YH) * NX + x) * grads_ref.shape[1]) // PROJ
    rate = [plan_ref[step_ref[i]] for i in range(CKPT)]
    own = plan_ref[step_ref[mine]]
    whole = rate[0] + rate[1] + rate[2] + rate[3]
    shape = (8, grads_ref.shape[1])
    weight = jnp.full(shape, own, jnp.float32) / jnp.full(shape, whole, jnp.float32)
    weight = weight * (CKPT / jnp.sqrt(jnp.full(shape, FEATURES, jnp.float32)))
    factor = jnp.sqrt(weight)[:1]
    out_ref[...] = (grads_ref[...].astype(jnp.float32) * factor).astype(jnp.bfloat16)
    for ref, dx in zip(quarter_refs, (0, 1, -1, 2)):
        q = ref.shape[0]
        first = pl.multiple_of(((x - dx + NX) % NX) * q, q)
        ref[...] = out_ref[pl.ds(first, q), :]


def scale(grads, lr_plan, ckpt_step):
    rows, width = grads.shape
    quarter = jax.ShapeDtypeStruct((rows // NX, width), jnp.bfloat16)
    return pl.pallas_call(
        scale_kernel,
        out_shape=[jax.ShapeDtypeStruct((rows, width), jnp.bfloat16)] + [quarter] * NX,
        in_specs=[SMEM, SMEM, VMEM],
        out_specs=[VMEM] * (1 + NX),
        name="scale",
    )(lr_plan, ckpt_step, grads)


def early_products(lefts, rights):
    rows, width = rights[0][0].shape
    q, nd, nk = rows // NX, len(lefts), len(rights[0])
    pieces = [r for block in rights for r in block]

    def kernel(*refs):
        left_in, right_in = refs[:nd], refs[nd : nd + len(pieces)]
        right, acc, left, lsem, rsem = refs[nd + len(pieces) :]
        lcopies = [pltpu.make_async_copy(left_in[i], left.at[i], lsem.at[i]) for i in range(nd)]
        rcopies = [
            pltpu.make_async_copy(
                right_in[i], right.at[i // nk, :, pl.ds(i % nk * width, width)], rsem.at[i]
            )
            for i in range(len(pieces))
        ]
        for copy in lcopies + rcopies:
            copy.start()
        for copy in lcopies:
            copy.wait()
        for block in range(4):
            total = 0.0
            for k in range(nk):
                rcopies[block * nk + k].wait()
                part = left[:, k * q : (k + 1) * q, :].reshape(nd * q, width)
                total = total + dot_t(part, right[block, :, k * width : (k + 1) * width])
            acc[block] = total

    return pl.pallas_call(
        kernel,
        out_shape=[
            jax.ShapeDtypeStruct((4, rows, nk * width), jnp.bfloat16),
            jax.ShapeDtypeStruct((4, nd * q, rows), jnp.float32),
        ],
        in_specs=[HBM] * (nd + len(pieces)),
        out_specs=[VMEM, VMEM],
        scratch_shapes=[
            pltpu.VMEM((nd, rows, width), jnp.bfloat16),
            pltpu.SemaphoreType.DMA((nd,)),
            pltpu.SemaphoreType.DMA((len(pieces),)),
        ],
        compiler_params=pltpu.CompilerParams(vmem_limit_bytes=32 * 2**20),
        cost_estimate=pl.CostEstimate(
            flops=2 * nd * q * 4 * rows * nk * width,
            bytes_accessed=2 * (nd + len(pieces)) * rows * width,
            transcendentals=0,
        ),
        name="early",
    )(*lefts, *pieces)


def late_products(right, acc, early, late, far, ds):
    rows, width = far[0].shape
    q, ne, nl = rows // NX, len(early), len(late)
    nk = NX - 1

    def kernel(right, acc, *refs):
        late_in, early_in, far_in = refs[:nl], refs[nl : nl + ne], refs[nl + ne : nl + ne + 4]
        out, left, tail, block_in, sums, sem = refs[nl + ne + 4 :]
        z, a, c = (lax.axis_index(n) for n in (Z, YL, C))
        moves = [(late_in[i], left.at[i]) for i in range(nl)]
        moves += [
            (early_in[i].at[pl.ds(nk * q, q)], tail.at[pl.ds(i * q, q)]) for i in range(ne)
        ]
        moves += [(far_in[i], block_in.at[i]) for i in range(4)]
        copies = [pltpu.make_async_copy(a, b, sem.at[i]) for i, (a, b) in enumerate(moves)]
        for copy in copies:
            copy.start()
        for copy in copies[:nl]:
            copy.wait()

        def part(k):
            return left[:, k * q : (k + 1) * q, :].reshape(nl * q, width)

        for block in range(4):
            total = 0.0
            for k in range(nk):
                total = total + dot_t(part(k), right[block, :, k * width : (k + 1) * width])
            sums[block] = total
        for copy in copies[nl:]:
            copy.wait()
        for block in range(4):
            ylo, core = (a + block // 2) % 2, (c + block % 2) % 2
            base = (ylo * 2 + core) * NZ
            first = (acc[block] + dot_t(tail[...], block_in[block])).astype(jnp.bfloat16)
            second = (sums[block] + dot_t(part(nk), block_in[block])).astype(jnp.bfloat16)
            for i, d in enumerate(ds):
                tile = first[i * q : (i + 1) * q] if i < ne else second[(i - ne) * q : (i - ne + 1) * q]
                out[base + (z + d + NZ) % NZ] = tile

    n_moves = 4 + ne + nl
    return pl.pallas_call(
        kernel,
        out_shape=jax.ShapeDtypeStruct((4 * NZ, q, rows), jnp.bfloat16),
        in_specs=[VMEM, VMEM] + [HBM] * n_moves,
        out_specs=VMEM,
        scratch_shapes=[
            pltpu.VMEM((nl, rows, width), jnp.bfloat16),
            pltpu.VMEM((ne * q, width), jnp.bfloat16),
            pltpu.VMEM((4, rows, width), jnp.bfloat16),
            pltpu.VMEM((4, nl * q, rows), jnp.float32),
            pltpu.SemaphoreType.DMA((n_moves,)),
        ],
        compiler_params=pltpu.CompilerParams(vmem_limit_bytes=32 * 2**20),
        cost_estimate=pl.CostEstimate(
            flops=2 * (nl * NX + ne) * q * 4 * rows * width,
            bytes_accessed=2 * n_moves * rows * width,
            transcendentals=0,
        ),
        name="late",
    )(right, acc, *late, *early, *far)


def after(values, done):
    return lax.optimization_barrier((tuple(values), tuple(done)))[0]


def on_device(grads, lr_plan, ckpt_step):
    c = lax.axis_index(C)
    s, *quarters = scale(grads, lr_plan, ckpt_step)
    rows = s.shape[0]
    swap = lambda v: take_from(v, C, 2, 1)

    heads = [take_from(v, X, NX, dx) for v, dx in zip(quarters[1:], (1, -1, 2))]
    other = take_from(s, YL, 2, 1)
    ring = {0: jnp.concatenate([quarters[0]] + heads, axis=0)}
    ring[1], ring[-1] = take_from(ring[0], Z, NZ, 1), take_from(ring[0], Z, NZ, -1)
    (ready,) = after((s,), heads)
    fs, bs = take_from(ready, X, NX, 1), take_from(ready, X, NX, -1)

    up, down = after((ring[1], ring[-1]), (fs, bs))
    ring[2], ring[-2] = take_from(up, Z, NZ, 1), take_from(down, Z, NZ, -1)
    (ready,) = after((other,), (fs, bs))
    fo, bo = take_from(ready, X, NX, 1), take_from(ready, X, NX, -1)

    up, down = after((ring[2], ring[-2]), (fo, bo))
    ring[3], ring[-3] = take_from(up, Z, NZ, 1), take_from(down, Z, NZ, -1)
    f_ready, b_ready = after((fs, bo), (fo, bo))
    far_s, far_o = take_from(f_ready, X, NX, 1), take_from(b_ready, X, NX, -1)

    ends = jnp.where(c == 0, ring[3], ring[-3])
    pairs = [((i + 1) % NZ * 2, i * 2) for i in range(NZ)]
    pairs += [(i * 2 + 1, (i + 1) % NZ * 2 + 1) for i in range(NZ)]
    ring[4] = lax.ppermute(ends, (Z, C), pairs)

    s_ready, o_ready = after((s, other), (fs, bs))
    far_s_ready, far_o_ready = after((far_s, far_o), (ring[3], ring[-3]))
    own = [[s, fs, bs], [other, fo, bo]]
    rights = [own[0], [swap(v) for v in (s_ready, fs, bs)], own[1], [swap(v) for v in (o_ready, fo, bo)]]
    far = [far_s, swap(far_s_ready), far_o, swap(far_o_ready)]

    first = [ring[d] for d in (0, 1, -1, 2, -2)]
    right, acc = early_products(first, rights)
    send = late_products(
        right, acc, first, [ring[3], ring[-3], ring[4]], far, (0, 1, -1, 2, -2, 3, -3, 4)
    )
    got = lax.all_to_all(send, (YL, C, YH, X), 0, 0)
    q = rows // NX
    got = got.reshape(2, 2, 2, NX, q, rows).astype(jnp.float32)
    total = got[:, :, 0] + got[:, :, 1]
    return total.reshape(2 * 2 * NX * q, rows).T


def solution(mesh):
    fine = Mesh(mesh.devices.reshape(NZ, 2, 2, 2, NX), (Z, YL, C, YH, X))
    spec = P((Z, YL, C), (YH, X))
    return jax.shard_map(
        on_device, mesh=fine, in_specs=(spec, P(), P()), out_specs=spec, check_vma=False
    )
```

time: 255 us -> 106 us (0.42)
  waiting for transfers between devices: 224 us -> 25.1 us
  starting transfers between devices: 0.04 us -> 38.8 us
  blocking collectives: 0 us -> 21.4 us
  matrix products: 13.7 us -> 0 us
  Pallas kernels: 0 us -> 13.7 us
  between operations: 13.4 us -> 0.16 us
  local copies, waits for them, and re-layouts: 0.01 us -> 5.15 us
  other arithmetic: 4.08 us -> 1.49 us
    reduce_scatter x1 -> x0, waiting for transfers between devices: 120 us -> none  [on_device(): lax.psum_scatter(partial_rows, 'feat', scatter_dimension=1, tiled=True)]
    all_gather x1 -> x0, waiting for transfers between devices: 104 us -> none  [on_device(): lax.all_gather(scaled, 'ex', axis=0, tiled=True)]
    ppermute x0 -> x25, starting transfers between devices: none -> 38.8 us  [the longest x24 38.8 us: take_from(): lax.ppermute(value, axis, [(i, (i - step) % size) for i in range(size)])]
    ppermute x0 -> x25, waiting for transfers between devices: none -> 25.1 us  [the longest x24 25.1 us: take_from(): lax.ppermute(value, axis, [(i, (i - step) % size) for i in range(size)])]
    all_to_all x0 -> x1, blocking collectives: none -> 21.4 us  [on_device(): got = lax.all_to_all(send, (YL, C, YH, X), 0, 0)]
    pallas_call x0 -> x3, Pallas kernels: none -> 13.7 us  [the longest x1 6.72 us: early_products(): pl.pallas_call(kernel, out_shape=[jax.ShapeDtypeStruct((4, rows, nk * wid...]
    dot_general x1 -> x0, matrix products: 13.7 us -> none  [pair_block(): lax.dot_general(rows_left, rows_right, (((1,), (1,)), ((), ())), preferre...]
    unnamed x0 -> x13, local copies, waits for them, and re-layouts: none -> 3.83 us
  transfers between devices with their start and end apart: 2 -> 25, of which waited for: 2 -> 8; matrix products, arithmetic and copies ran while one was open for 0% -> 2% of each run, Pallas kernels for 0% -> 6%
where the time goes in v1:
time: 106 us
  starting transfers between devices  38.8 us (37%)
  waiting for transfers between devices  25.1 us (24%)
  blocking collectives  21.4 us (20%)
  Pallas kernels  13.7 us (13%)
  local copies, waits for them, and re-layouts  5.15 us (5%)
  other arithmetic  1.49 us (1%)
    ppermute x24, starting transfers between devices, take_from(): lax.ppermute(value, axis, [(i, (i - step) % size) for i in range(size)])  38.8 us
    ppermute x24, waiting for transfers between devices, take_from(): lax.ppermute(value, axis, [(i, (i - step) % size) for i in range(size)])  25.1 us
    all_to_all x1, blocking collectives, on_device(): got = lax.all_to_all(send, (YL, C, YH, X), 0, 0)  21.4 us
    pallas_call x1, Pallas kernels, early_products(): pl.pallas_call(kernel, out_shape=[jax.ShapeDtypeStruct((4, rows, nk * wid...  6.72 us
    pallas_call x1, Pallas kernels, late_products(): pl.pallas_call(kernel, out_shape=jax.ShapeDtypeStruct((4 * NZ, q, rows),...  4.83 us
    unnamed x13, local copies, waits for them, and re-layouts  3.83 us
    pallas_call x1, Pallas kernels, scale(): pl.pallas_call(scale_kernel, out_shape=[jax.ShapeDtypeStruct((rows, width...  2.19 us
  transfers between devices with their start and end apart: 25, of which 8 were waited for; matrix products, arithmetic and copies ran while one was open for 2% of the time, Pallas kernels for 6%

profile of v1, /device:TPU:1, one launch (start us, length us, event | category | flops | bytes accessed | tf_op | source)
XLA Modules:
  0.0 105.8 jit_solution(7312161200403974568)
XLA Ops:
  0.0 2.2 %scale.1 = (bf16[256,1024]{1,0:T(8,128)(2,1)}, bf16[64,1024]{1,0:T(8,128)(2,1)}, bf16[64,1024]{1,0:T(8,128)(2,1)}, bf16[64,1024]{1,0:T(8,128)(2,1)}, bf16[64,1024]{1,0:T(8,128)(2,1)}) custom-call(f32[64]{0:T(128)} %plan_ref.1, s32[4]{0:T(128)} %step_ref.1, bf16[256,1024]{1,0:T(8,128)(2,1)} %grads_ref.1), custom_call_target="tpu_custom_call" | custom-call | tf_op jit(solution)/shard_map/scale/pallas_call | solution.py:47
  2.2 3.3 %collective-permute-start = (bf16[64,1024]{1,0:T(8,128)(2,1)}, bf16[64,1024]{1,0:T(8,128)(2,1)S(1)}, u32[]{:S(2)}, u32[]{:S(2)}) collective-permute-start(bf16[64,1024]{1,0:T(8,128)(2,1)} %get-tuple-element.25), channel_id=1, source_target_pairs={{0,3},{1,0},{2,1},{3,2},{4,7},{5,4},{6,5},{7,6},{8,11},{9,8},{10,9... | collective-permute-start | bytes 393224 | tf_op jit(solution)/shard_map/ppermute | solution.py:20
  5.5 0.0 collective-permute-start.1
  5.5 1.7 %collective-permute-start.2 = (bf16[64,1024]{1,0:T(8,128)(2,1)}, bf16[64,1024]{1,0:T(8,128)(2,1)S(1)}, u32[]{:S(2)}, u32[]{:S(2)}) collective-permute-start(bf16[64,1024]{1,0:T(8,128)(2,1)} %get-tuple-element.27), channel_id=1, source_target_pairs={{0,2},{1,3},{2,0},{3,1},{4,6},{5,7},{6,4},{7,5},{8,10},{9,11},{10,... | collective-permute-start | bytes 393224 | tf_op jit(solution)/shard_map/ppermute | solution.py:20
  7.2 0.9 constant_dynamic-update-slice_fusion.3
  8.1 0.0 collective-permute-done
  8.2 4.7 %collective-permute-done.1 = bf16[64,1024]{1,0:T(8,128)(2,1)S(1)} collective-permute-done((bf16[64,1024]{1,0:T(8,128)(2,1)}, bf16[64,1024]{1,0:T(8,128)(2,1)S(1)}, u32[]{:S(2)}, u32[]{:S(2)}) %collective-permute-start.1) | collective-permute-done | bytes 131104 | tf_op jit(solution)/shard_map/ppermute | solution.py:20
  12.9 0.0 collective-permute-done.2
  12.9 5.7 %collective-permute-start.3 = (bf16[256,1024]{1,0:T(8,128)(2,1)S(1)}, bf16[256,1024]{1,0:T(8,128)(2,1)S(1)}, u32[]{:S(2)}, u32[]{:S(2)}) collective-permute-start(bf16[256,1024]{1,0:T(8,128)(2,1)S(1)} %constant_dynamic-update-slice_fusion.refs_0_.refs_3_), channel_id=1, source_target_pairs={{0,224},{32,0},{64,32},{96,64},{128,96},{160,128},{192,160},{224,1... | collective-permute-start | bytes 1572872 | tf_op jit(solution)/shard_map/ppermute | solution.py:20
  18.6 0.0 collective-permute-start.4
  18.6 0.8 collective-permute-start.5
  19.4 0.7 collective-permute-start.6
  20.0 1.3 %collective-permute-start.9 = (bf16[256,1024]{1,0:T(8,128)(2,1)}, bf16[256,1024]{1,0:T(8,128)(2,1)}, u32[]{:S(2)}, u32[]{:S(2)}) collective-permute-start(bf16[256,1024]{1,0:T(8,128)(2,1)} %get-tuple-element.32.refs_5_), channel_id=1, source_target_pairs={{0,16},{16,0},{1,17},{17,1},{2,18},{18,2},{3,19},{19,3},{4,20},{20... | collective-permute-start | bytes 1572872 | tf_op jit(solution)/shard_map/ppermute | solution.py:20
  21.3 5.7 %collective-permute-done.3.refs_1_.refs_4_ = bf16[256,1024]{1,0:T(8,128)(2,1)S(1)} collective-permute-done((bf16[256,1024]{1,0:T(8,128)(2,1)S(1)}, bf16[256,1024]{1,0:T(8,128)(2,1)S(1)}, u32[]{:S(2)}, u32[]{:S(2)}) %collective-permute-start.3) | collective-permute-done | bytes 524320 | tf_op jit(solution)/shard_map/ppermute | solution.py:20
  27.0 3.2 %collective-permute-done.4.refs_2_.refs_5_ = bf16[256,1024]{1,0:T(8,128)(2,1)S(1)} collective-permute-done((bf16[256,1024]{1,0:T(8,128)(2,1)S(1)}, bf16[256,1024]{1,0:T(8,128)(2,1)S(1)}, u32[]{:S(2)}, u32[]{:S(2)}) %collective-permute-start.4) | collective-permute-done | bytes 524320 | tf_op jit(solution)/shard_map/ppermute | solution.py:20
  30.3 0.0 collective-permute-done.5.refs_6_
  30.3 1.1 %collective-permute-done.6.refs_7_ = bf16[256,1024]{1,0:T(8,128)(2,1)} collective-permute-done((bf16[256,1024]{1,0:T(8,128)(2,1)}, bf16[256,1024]{1,0:T(8,128)(2,1)}, u32[]{:S(2)}, u32[]{:S(2)}) %collective-permute-start.6) | collective-permute-done | bytes 524320 | tf_op jit(solution)/shard_map/ppermute | solution.py:20
  31.4 2.4 %collective-permute-start.7 = (bf16[256,1024]{1,0:T(8,128)(2,1)S(1)}, bf16[256,1024]{1,0:T(8,128)(2,1)S(1)}, u32[]{:S(2)}, u32[]{:S(2)}) collective-permute-start(bf16[256,1024]{1,0:T(8,128)(2,1)S(1)} %collective-permute-done.3.refs_1_.refs_4_), channel_id=1, source_target_pairs={{0,224},{32,0},{64,32},{96,64},{128,96},{160,128},{192,160},{224,1... | collective-permute-start | bytes 1572872 | tf_op jit(solution)/shard_map/ppermute | solution.py:20
  33.8 0.0 collective-permute-start.8
  33.8 0.0 collective-permute-done.9.refs_11_
  33.8 0.7 collective-permute-start.13
  34.5 0.7 collective-permute-start.14
  35.2 5.7 %collective-permute-done.7.refs_3_.refs_6_ = bf16[256,1024]{1,0:T(8,128)(2,1)S(1)} collective-permute-done((bf16[256,1024]{1,0:T(8,128)(2,1)S(1)}, bf16[256,1024]{1,0:T(8,128)(2,1)S(1)}, u32[]{:S(2)}, u32[]{:S(2)}) %collective-permute-start.7) | collective-permute-done | bytes 524320 | tf_op jit(solution)/shard_map/ppermute | solution.py:20
  40.9 3.1 %collective-permute-done.8.refs_4_.refs_7_ = bf16[256,1024]{1,0:T(8,128)(2,1)S(1)} collective-permute-done((bf16[256,1024]{1,0:T(8,128)(2,1)S(1)}, bf16[256,1024]{1,0:T(8,128)(2,1)S(1)}, u32[]{:S(2)}, u32[]{:S(2)}) %collective-permute-start.8) | collective-permute-done | bytes 524320 | tf_op jit(solution)/shard_map/ppermute | solution.py:20
  44.1 0.0 collective-permute-done.13.refs_12_
  44.1 1.4 %collective-permute-done.14.refs_13_ = bf16[256,1024]{1,0:T(8,128)(2,1)} collective-permute-done((bf16[256,1024]{1,0:T(8,128)(2,1)}, bf16[256,1024]{1,0:T(8,128)(2,1)}, u32[]{:S(2)}, u32[]{:S(2)}) %collective-permute-start.14) | collective-permute-done | bytes 524320 | tf_op jit(solution)/shard_map/ppermute | solution.py:20
  45.5 0.0 copy-done.3
  45.5 2.4 %collective-permute-start.18 = (bf16[256,1024]{1,0:T(8,128)(2,1)S(1)}, bf16[256,1024]{1,0:T(8,128)(2,1)S(1)}, u32[]{:S(2)}, u32[]{:S(2)}) collective-permute-start(bf16[256,1024]{1,0:T(8,128)(2,1)S(1)} %collective-permute-done.7.refs_3_.refs_6_), channel_id=1, source_target_pairs={{0,224},{32,0},{64,32},{96,64},{128,96},{160,128},{192,160},{224,1... | collective-permute-start | bytes 1572872 | tf_op jit(solution)/shard_map/ppermute | solution.py:20
  47.9 0.0 collective-permute-start.19
  47.9 1.0 collective-permute-start.21
  48.9 0.5 collective-permute-start.22
  49.3 6.0 %collective-permute-start.10 = (bf16[256,1024]{1,0:T(8,128)(2,1)}, bf16[256,1024]{1,0:T(8,128)(2,1)}, u32[]{:S(2)}, u32[]{:S(2)}) collective-permute-start(bf16[256,1024]{1,0:T(8,128)(2,1)} %get-tuple-element.32.refs_5_), channel_id=1, source_target_pairs={{0,8},{8,0},{1,9},{9,1},{2,10},{10,2},{3,11},{11,3},{4,12},{12,4},... | collective-permute-start | bytes 1572872 | tf_op jit(solution)/shard_map/ppermute | solution.py:20
  55.4 0.0 collective-permute-done.18.refs_0_
  55.4 4.7 %collective-permute-start.11 = (bf16[256,1024]{1,0:T(8,128)(2,1)}, bf16[256,1024]{1,0:T(8,128)(2,1)}, u32[]{:S(2)}, u32[]{:S(2)}) collective-permute-start(bf16[256,1024]{1,0:T(8,128)(2,1)} %collective-permute-done.5.refs_6_), channel_id=1, source_target_pairs={{0,8},{8,0},{1,9},{9,1},{2,10},{10,2},{3,11},{11,3},{4,12},{12,4},... | collective-permute-start | bytes 1572872 | tf_op jit(solution)/shard_map/ppermute | solution.py:20
  60.0 0.0 collective-permute-done.19.refs_1_
  60.0 0.8 copy-done
  60.9 3.7 %collective-permute-start.12 = (bf16[256,1024]{1,0:T(8,128)(2,1)}, bf16[256,1024]{1,0:T(8,128)(2,1)}, u32[]{:S(2)}, u32[]{:S(2)}) collective-permute-start(bf16[256,1024]{1,0:T(8,128)(2,1)} %collective-permute-done.6.refs_7_), channel_id=1, source_target_pairs={{0,8},{8,0},{1,9},{9,1},{2,10},{10,2},{3,11},{11,3},{4,12},{12,4},... | collective-permute-start | bytes 1572872 | tf_op jit(solution)/shard_map/ppermute | solution.py:20
  64.5 0.0 collective-permute-done.21.refs_8_
  64.5 0.0 collective-permute-start.15
  64.6 0.0 collective-permute-done.22.refs_10_
  64.6 0.5 collective-permute-start.16
  65.1 0.0 collective-permute-done.10.refs_8_
  65.1 0.1 collective-permute-start.17
  65.2 1.1 %broadcast_select_fusion = bf16[256,1024]{1,0:T(8,128)(2,1)S(1)} fusion(bf16[256,1024]{1,0:T(8,128)(2,1)S(1)} %collective-permute-done.18.refs_0_, bf16[256,1024]{1,0:T(8,128)(2,1)} %copy-done, pred[]{:T(512)S(6)} %eq.3), kind=kLoop, calls=%fused_computation.3 | loop fusion | flops 262144 | bytes 1572865 | tf_op jit(solution)/shard_map/jit(_where)/select_n | solution.py:195
  66.3 0.0 copy-start.1
  66.3 0.0 collective-permute-done.11.refs_9_
  66.3 0.1 collective-permute-start.20
  66.4 0.1 collective-permute-done.12.refs_10_
  66.4 2.5 %collective-permute-start.23 = (bf16[256,1024]{1,0:T(8,128)(2,1)}, bf16[256,1024]{1,0:T(8,128)(2,1)S(1)}, u32[]{:S(2)}, u32[]{:S(2)}) collective-permute-start(bf16[256,1024]{1,0:T(8,128)(2,1)} %collective-permute-done.21.refs_8_), channel_id=1, source_target_pairs={{0,8},{8,0},{1,9},{9,1},{2,10},{10,2},{3,11},{11,3},{4,12},{12,4},... | collective-permute-start | bytes 1572872 | tf_op jit(solution)/shard_map/ppermute | solution.py:20
  68.9 0.0 collective-permute-done.15.refs_14_
  68.9 0.1 collective-permute-start.24
  69.0 0.0 collective-permute-done.16.refs_15_
  69.0 0.0 collective-permute-done.17.refs_16_
  69.0 1.0 copy-done.2
  70.1 1.0 copy-done.4
  71.1 6.7 %early.1 = (bf16[4,256,3072]{2,1,0:T(8,128)(2,1)S(1)}, f32[4,320,256]{2,1,0:T(8,128)S(1)}) custom-call(bf16[256,1024]{1,0:T(8,128)(2,1)S(1)} %constant_dynamic-update-slice_fusion.refs_0_.refs_3_, bf16[256,1024]{1,0:T(8,128)(2,1)S(1)} %collective-permute-done.3.refs_1_.refs_4_, bf16[256,1024]{1,0:T(8,128)(2,1)S(1)} %collective-permute-done.4.refs_2_.refs_5_, ...), custom_call_target="tpu_custom_call" | custom-call | flops 2013265920 | bytes 8912896 | tf_op jit(solution)/shard_map/early/pallas_call | solution.py:83
  77.9 0.0 collective-permute-done.20.refs_2_
  77.9 0.0 collective-permute-done.23.refs_9_
  77.9 0.0 collective-permute-done.24.refs_11_
  77.9 4.8 %late.1 = bf16[32,64,256]{2,1,0:T(8,128)(2,1)S(1)} custom-call(bf16[4,256,3072]{2,1,0:T(8,128)(2,1)S(1)} %get-tuple-element.35.right, f32[4,320,256]{2,1,0:T(8,128)S(1)} %get-tuple-element.36.acc, bf16[256,1024]{1,0:T(8,128)(2,1)S(1)} %collective-permute-done.18.refs_0_, bf16[256,1024]{1,0:T(8,128)(2,1)S(1)} %copy-done.1, ...), custom_call_target="tpu_custom_call" | custom-call | flops 2281701376 | bytes 6291456 | tf_op jit(solution)/shard_map/late/pallas_call | solution.py:146
  82.7 21.4 %all_to_all.5 = bf16[32,64,256]{2,1,0:T(8,128)(2,1)S(1)} all-to-all(bf16[32,64,256]{2,1,0:T(8,128)(2,1)S(1)} %late.1), channel_id=1, replica_groups=mesh['z'=8,'ylo'=2,'core'=2,'yhi'=2,'x'=4] {'ylo','core','yhi','x'}, dimensions={0} | all-to-all | bytes 2097152 | tf_op jit(solution)/shard_map/all_to_all | solution.py:211
  104.1 0.2 convert.1
  104.3 0.2 fusion
  104.5 1.3 %copy.7 = f32[256,1024]{1,0:T(8,128)} copy(f32[256,1024]{0,1:T(8,128)S(1)} %bitcast.14) | data formatting | bytes 2097152 | tf_op jit(solution)/shard_map/transpose | solution.py:215
  (8 shorter events, 0.0 us)
Async XLA Ops:
  2.2 6.0 %collective-permute-start = (bf16[64,1024]{1,0:T(8,128)(2,1)}, bf16[64,1024]{1,0:T(8,128)(2,1)S(1)}, u32[]{:S(2)}, u32[]{:S(2)}) collective-permute-start(bf16[64,1024]{1,0:T(8,128)(2,1)} %get-tuple-element.25), channel_id=1, source_target_pairs={{0,3},{1,0},{2,1},{3,2},{4,7},{5,4},{6,5},{7,6},{8,11},{9,8},{10,9... | collective-permute-start | bytes 393224 | tf_op jit(solution)/shard_map/ppermute | solution.py:20
  5.5 7.4 %collective-permute-start.1 = (bf16[64,1024]{1,0:T(8,128)(2,1)}, bf16[64,1024]{1,0:T(8,128)(2,1)S(1)}, u32[]{:S(2)}, u32[]{:S(2)}) collective-permute-start(bf16[64,1024]{1,0:T(8,128)(2,1)} %get-tuple-element.26), channel_id=1, source_target_pairs={{0,1},{1,2},{2,3},{3,0},{4,5},{5,6},{6,7},{7,4},{8,9},{9,10},{10,1... | collective-permute-start | bytes 393224 | tf_op jit(solution)/shard_map/ppermute | solution.py:20
  5.5 7.4 %collective-permute-start.2 = (bf16[64,1024]{1,0:T(8,128)(2,1)}, bf16[64,1024]{1,0:T(8,128)(2,1)S(1)}, u32[]{:S(2)}, u32[]{:S(2)}) collective-permute-start(bf16[64,1024]{1,0:T(8,128)(2,1)} %get-tuple-element.27), channel_id=1, source_target_pairs={{0,2},{1,3},{2,0},{3,1},{4,6},{5,7},{6,4},{7,5},{8,10},{9,11},{10,... | collective-permute-start | bytes 393224 | tf_op jit(solution)/shard_map/ppermute | solution.py:20
  12.9 14.1 %collective-permute-start.3 = (bf16[256,1024]{1,0:T(8,128)(2,1)S(1)}, bf16[256,1024]{1,0:T(8,128)(2,1)S(1)}, u32[]{:S(2)}, u32[]{:S(2)}) collective-permute-start(bf16[256,1024]{1,0:T(8,128)(2,1)S(1)} %constant_dynamic-update-slice_fusion.refs_0_.refs_3_), channel_id=1, source_target_pairs={{0,224},{32,0},{64,32},{96,64},{128,96},{160,128},{192,160},{224,1... | collective-permute-start | bytes 1572872 | tf_op jit(solution)/shard_map/ppermute | solution.py:20
  18.6 11.7 %collective-permute-start.4 = (bf16[256,1024]{1,0:T(8,128)(2,1)S(1)}, bf16[256,1024]{1,0:T(8,128)(2,1)S(1)}, u32[]{:S(2)}, u32[]{:S(2)}) collective-permute-start(bf16[256,1024]{1,0:T(8,128)(2,1)S(1)} %constant_dynamic-update-slice_fusion.refs_0_.refs_3_), channel_id=1, source_target_pairs={{0,32},{32,64},{64,96},{96,128},{128,160},{160,192},{192,224},{224... | collective-permute-start | bytes 1572872 | tf_op jit(solution)/shard_map/ppermute | solution.py:20
  18.6 11.7 %collective-permute-start.5 = (bf16[256,1024]{1,0:T(8,128)(2,1)}, bf16[256,1024]{1,0:T(8,128)(2,1)}, u32[]{:S(2)}, u32[]{:S(2)}) collective-permute-start(bf16[256,1024]{1,0:T(8,128)(2,1)} %get-tuple-element.32.refs_5_), channel_id=1, source_target_pairs={{0,3},{1,0},{2,1},{3,2},{4,7},{5,4},{6,5},{7,6},{8,11},{9,8},{10,9... | collective-permute-start | bytes 1572872 | tf_op jit(solution)/shard_map/ppermute | solution.py:20
  19.4 12.0 %collective-permute-start.6 = (bf16[256,1024]{1,0:T(8,128)(2,1)}, bf16[256,1024]{1,0:T(8,128)(2,1)}, u32[]{:S(2)}, u32[]{:S(2)}) collective-permute-start(bf16[256,1024]{1,0:T(8,128)(2,1)} %get-tuple-element.32.refs_5_), channel_id=1, source_target_pairs={{0,1},{1,2},{2,3},{3,0},{4,5},{5,6},{6,7},{7,4},{8,9},{9,10},{10,1... | collective-permute-start | bytes 1572872 | tf_op jit(solution)/shard_map/ppermute | solution.py:20
  20.0 13.7 %collective-permute-start.9 = (bf16[256,1024]{1,0:T(8,128)(2,1)}, bf16[256,1024]{1,0:T(8,128)(2,1)}, u32[]{:S(2)}, u32[]{:S(2)}) collective-permute-start(bf16[256,1024]{1,0:T(8,128)(2,1)} %get-tuple-element.32.refs_5_), channel_id=1, source_target_pairs={{0,16},{16,0},{1,17},{17,1},{2,18},{18,2},{3,19},{19,3},{4,20},{20... | collective-permute-start | bytes 1572872 | tf_op jit(solution)/shard_map/ppermute | solution.py:20
  31.4 9.6 %collective-permute-start.7 = (bf16[256,1024]{1,0:T(8,128)(2,1)S(1)}, bf16[256,1024]{1,0:T(8,128)(2,1)S(1)}, u32[]{:S(2)}, u32[]{:S(2)}) collective-permute-start(bf16[256,1024]{1,0:T(8,128)(2,1)S(1)} %collective-permute-done.3.refs_1_.refs_4_), channel_id=1, source_target_pairs={{0,224},{32,0},{64,32},{96,64},{128,96},{160,128},{192,160},{224,1... | collective-permute-start | bytes 1572872 | tf_op jit(solution)/shard_map/ppermute | solution.py:20
  33.8 10.3 %collective-permute-start.8 = (bf16[256,1024]{1,0:T(8,128)(2,1)S(1)}, bf16[256,1024]{1,0:T(8,128)(2,1)S(1)}, u32[]{:S(2)}, u32[]{:S(2)}) collective-permute-start(bf16[256,1024]{1,0:T(8,128)(2,1)S(1)} %collective-permute-done.4.refs_2_.refs_5_), channel_id=1, source_target_pairs={{0,32},{32,64},{64,96},{96,128},{128,160},{160,192},{192,224},{224... | collective-permute-start | bytes 1572872 | tf_op jit(solution)/shard_map/ppermute | solution.py:20
  33.8 10.3 %collective-permute-start.13 = (bf16[256,1024]{1,0:T(8,128)(2,1)}, bf16[256,1024]{1,0:T(8,128)(2,1)S(1)}, u32[]{:S(2)}, u32[]{:S(2)}) collective-permute-start(bf16[256,1024]{1,0:T(8,128)(2,1)} %collective-permute-done.9.refs_11_), channel_id=1, source_target_pairs={{0,3},{1,0},{2,1},{3,2},{4,7},{5,4},{6,5},{7,6},{8,11},{9,8},{10,9... | collective-permute-start | bytes 1572872 | tf_op jit(solution)/shard_map/ppermute | solution.py:20
  34.5 11.0 %collective-permute-start.14 = (bf16[256,1024]{1,0:T(8,128)(2,1)}, bf16[256,1024]{1,0:T(8,128)(2,1)}, u32[]{:S(2)}, u32[]{:S(2)}) collective-permute-start(bf16[256,1024]{1,0:T(8,128)(2,1)} %collective-permute-done.9.refs_11_), channel_id=1, source_target_pairs={{0,1},{1,2},{2,3},{3,0},{4,5},{5,6},{6,7},{7,4},{8,9},{9,10},{10,1... | collective-permute-start | bytes 1572872 | tf_op jit(solution)/shard_map/ppermute | solution.py:20
  44.1 1.4 %copy-start.3 = (bf16[256,1024]{1,0:T(8,128)(2,1)}, bf16[256,1024]{1,0:T(8,128)(2,1)S(1)}, u32[]{:S(2)}) copy-start(bf16[256,1024]{1,0:T(8,128)(2,1)S(1)} %collective-permute-done.13.refs_12_) | copy-start | bytes 1572868
  45.5 9.9 %collective-permute-start.18 = (bf16[256,1024]{1,0:T(8,128)(2,1)S(1)}, bf16[256,1024]{1,0:T(8,128)(2,1)S(1)}, u32[]{:S(2)}, u32[]{:S(2)}) collective-permute-start(bf16[256,1024]{1,0:T(8,128)(2,1)S(1)} %collective-permute-done.7.refs_3_.refs_6_), channel_id=1, source_target_pairs={{0,224},{32,0},{64,32},{96,64},{128,96},{160,128},{192,160},{224,1... | collective-permute-start | bytes 1572872 | tf_op jit(solution)/shard_map/ppermute | solution.py:20
  47.9 12.2 %collective-permute-start.19 = (bf16[256,1024]{1,0:T(8,128)(2,1)S(1)}, bf16[256,1024]{1,0:T(8,128)(2,1)S(1)}, u32[]{:S(2)}, u32[]{:S(2)}) collective-permute-start(bf16[256,1024]{1,0:T(8,128)(2,1)S(1)} %collective-permute-done.8.refs_4_.refs_7_), channel_id=1, source_target_pairs={{0,32},{32,64},{64,96},{96,128},{128,160},{160,192},{192,224},{224... | collective-permute-start | bytes 1572872 | tf_op jit(solution)/shard_map/ppermute | solution.py:20
  47.9 16.7 %collective-permute-start.21 = (bf16[256,1024]{1,0:T(8,128)(2,1)}, bf16[256,1024]{1,0:T(8,128)(2,1)}, u32[]{:S(2)}, u32[]{:S(2)}) collective-permute-start(bf16[256,1024]{1,0:T(8,128)(2,1)} %collective-permute-done.5.refs_6_), channel_id=1, source_target_pairs={{0,3},{1,0},{2,1},{3,2},{4,7},{5,4},{6,5},{7,6},{8,11},{9,8},{10,9... | collective-permute-start | bytes 1572872 | tf_op jit(solution)/shard_map/ppermute | solution.py:20
  48.9 15.7 %collective-permute-start.22 = (bf16[256,1024]{1,0:T(8,128)(2,1)}, bf16[256,1024]{1,0:T(8,128)(2,1)}, u32[]{:S(2)}, u32[]{:S(2)}) collective-permute-start(bf16[256,1024]{1,0:T(8,128)(2,1)} %collective-permute-done.14.refs_13_), channel_id=1, source_target_pairs={{0,1},{1,2},{2,3},{3,0},{4,5},{5,6},{6,7},{7,4},{8,9},{9,10},{10,1... | collective-permute-start | bytes 1572872 | tf_op jit(solution)/shard_map/ppermute | solution.py:20
  49.3 15.7 %collective-permute-start.10 = (bf16[256,1024]{1,0:T(8,128)(2,1)}, bf16[256,1024]{1,0:T(8,128)(2,1)}, u32[]{:S(2)}, u32[]{:S(2)}) collective-permute-start(bf16[256,1024]{1,0:T(8,128)(2,1)} %get-tuple-element.32.refs_5_), channel_id=1, source_target_pairs={{0,8},{8,0},{1,9},{9,1},{2,10},{10,2},{3,11},{11,3},{4,12},{12,4},... | collective-permute-start | bytes 1572872 | tf_op jit(solution)/shard_map/ppermute | solution.py:20
  55.4 10.9 %collective-permute-start.11 = (bf16[256,1024]{1,0:T(8,128)(2,1)}, bf16[256,1024]{1,0:T(8,128)(2,1)}, u32[]{:S(2)}, u32[]{:S(2)}) collective-permute-start(bf16[256,1024]{1,0:T(8,128)(2,1)} %collective-permute-done.5.refs_6_), channel_id=1, source_target_pairs={{0,8},{8,0},{1,9},{9,1},{2,10},{10,2},{3,11},{11,3},{4,12},{12,4},... | collective-permute-start | bytes 1572872 | tf_op jit(solution)/shard_map/ppermute | solution.py:20
  60.0 0.8 copy-start
  60.9 5.6 %collective-permute-start.12 = (bf16[256,1024]{1,0:T(8,128)(2,1)}, bf16[256,1024]{1,0:T(8,128)(2,1)}, u32[]{:S(2)}, u32[]{:S(2)}) collective-permute-start(bf16[256,1024]{1,0:T(8,128)(2,1)} %collective-permute-done.6.refs_7_), channel_id=1, source_target_pairs={{0,8},{8,0},{1,9},{9,1},{2,10},{10,2},{3,11},{11,3},{4,12},{12,4},... | collective-permute-start | bytes 1572872 | tf_op jit(solution)/shard_map/ppermute | solution.py:20
  64.5 4.4 %collective-permute-start.15 = (bf16[256,1024]{1,0:T(8,128)(2,1)}, bf16[256,1024]{1,0:T(8,128)(2,1)}, u32[]{:S(2)}, u32[]{:S(2)}) collective-permute-start(bf16[256,1024]{1,0:T(8,128)(2,1)} %collective-permute-done.9.refs_11_), channel_id=1, source_target_pairs={{0,8},{8,0},{1,9},{9,1},{2,10},{10,2},{3,11},{11,3},{4,12},{12,4},... | collective-permute-start | bytes 1572872 | tf_op jit(solution)/shard_map/ppermute | solution.py:20
  64.6 4.5 %collective-permute-start.16 = (bf16[256,1024]{1,0:T(8,128)(2,1)}, bf16[256,1024]{1,0:T(8,128)(2,1)S(1)}, u32[]{:S(2)}, u32[]{:S(2)}) collective-permute-start(bf16[256,1024]{1,0:T(8,128)(2,1)} %copy-done.3), channel_id=1, source_target_pairs={{0,8},{8,0},{1,9},{9,1},{2,10},{10,2},{3,11},{11,3},{4,12},{12,4},... | collective-permute-start | bytes 1572872 | tf_op jit(solution)/shard_map/ppermute | solution.py:20
  65.1 4.0 %collective-permute-start.17 = (bf16[256,1024]{1,0:T(8,128)(2,1)}, bf16[256,1024]{1,0:T(8,128)(2,1)S(1)}, u32[]{:S(2)}, u32[]{:S(2)}) collective-permute-start(bf16[256,1024]{1,0:T(8,128)(2,1)} %collective-permute-done.14.refs_13_), channel_id=1, source_target_pairs={{0,8},{8,0},{1,9},{9,1},{2,10},{10,2},{3,11},{11,3},{4,12},{12,4},... | collective-permute-start | bytes 1572872 | tf_op jit(solution)/shard_map/ppermute | solution.py:20
  66.3 11.6 %copy-start.1 = (bf16[256,1024]{1,0:T(8,128)(2,1)S(1)}, bf16[256,1024]{1,0:T(8,128)(2,1)}, u32[]{:S(2)}) copy-start(bf16[256,1024]{1,0:T(8,128)(2,1)} %copy-done) | copy-start | bytes 1572868
  66.3 11.6 %collective-permute-start.20 = (bf16[256,1024]{1,0:T(8,128)(2,1)S(1)}, bf16[256,1024]{1,0:T(8,128)(2,1)S(1)}, u32[]{:S(2)}, u32[]{:S(2)}) collective-permute-start(bf16[256,1024]{1,0:T(8,128)(2,1)S(1)} %broadcast_select_fusion), channel_id=1, source_target_pairs={{32,0},{64,32},{96,64},{128,96},{160,128},{192,160},{224,192},{0,2... | collective-permute-start | bytes 1572872 | tf_op jit(solution)/shard_map/ppermute | solution.py:198
  66.4 11.4 %collective-permute-start.23 = (bf16[256,1024]{1,0:T(8,128)(2,1)}, bf16[256,1024]{1,0:T(8,128)(2,1)S(1)}, u32[]{:S(2)}, u32[]{:S(2)}) collective-permute-start(bf16[256,1024]{1,0:T(8,128)(2,1)} %collective-permute-done.21.refs_8_), channel_id=1, source_target_pairs={{0,8},{8,0},{1,9},{9,1},{2,10},{10,2},{3,11},{11,3},{4,12},{12,4},... | collective-permute-start | bytes 1572872 | tf_op jit(solution)/shard_map/ppermute | solution.py:20
  68.9 8.9 %collective-permute-start.24 = (bf16[256,1024]{1,0:T(8,128)(2,1)}, bf16[256,1024]{1,0:T(8,128)(2,1)S(1)}, u32[]{:S(2)}, u32[]{:S(2)}) collective-permute-start(bf16[256,1024]{1,0:T(8,128)(2,1)} %collective-permute-done.22.refs_10_), channel_id=1, source_target_pairs={{0,8},{8,0},{1,9},{9,1},{2,10},{10,2},{3,11},{11,3},{4,12},{12,4},... | collective-permute-start | bytes 1572872 | tf_op jit(solution)/shard_map/ppermute | solution.py:20
  69.0 1.0 copy-start.2
  70.1 1.0 copy-start.4

commit v2 on v1

v2 whole, which is shorter than its diff:
```python
import jax
import jax.numpy as jnp
from jax import lax
from jax.experimental import pallas as pl
from jax.experimental.pallas import tpu as pltpu
from jax.sharding import Mesh, PartitionSpec as P

PROJ = 2048
CKPT = 4
FEATURES = 8192

Z, YL, C, YH, X = "z", "ylo", "core", "yhi", "x"
NZ, NX = 8, 4
SMEM = pl.BlockSpec(memory_space=pltpu.SMEM)
VMEM = pl.BlockSpec(memory_space=pltpu.VMEM)
HBM = pl.BlockSpec(memory_space=pltpu.HBM)


def take_from(value, axis, size, step):
    return lax.ppermute(value, axis, [(i, (i - step) % size) for i in range(size)])


def dot_t(left, right):
    return lax.dot_general(left, right, (((1,), (1,)), ((), ())), preferred_element_type=jnp.float32)


def scale_kernel(plan_ref, step_ref, grads_ref, out_ref, *quarter_refs):
    x = lax.axis_index(X)
    mine = ((lax.axis_index(YH) * NX + x) * grads_ref.shape[1]) // PROJ
    rate = [plan_ref[step_ref[i]] for i in range(CKPT)]
    own = plan_ref[step_ref[mine]]
    whole = rate[0] + rate[1] + rate[2] + rate[3]
    shape = (8, grads_ref.shape[1])
    weight = jnp.full(shape, own, jnp.float32) / jnp.full(shape, whole, jnp.float32)
    weight = weight * (CKPT / jnp.sqrt(jnp.full(shape, FEATURES, jnp.float32)))
    factor = jnp.sqrt(weight)[:1]
    out_ref[...] = (grads_ref[...].astype(jnp.float32) * factor).astype(jnp.bfloat16)
    for ref, dx in zip(quarter_refs, (0, 1, -1, 2)):
        q = ref.shape[0]
        first = pl.multiple_of(((x - dx + NX) % NX) * q, q)
        ref[...] = out_ref[pl.ds(first, q), :]


def scale(grads, lr_plan, ckpt_step):
    rows, width = grads.shape
    quarter = jax.ShapeDtypeStruct((rows // NX, width), jnp.bfloat16)
    return pl.pallas_call(
        scale_kernel,
        out_shape=[jax.ShapeDtypeStruct((rows, width), jnp.bfloat16)] + [quarter] * NX,
        in_specs=[SMEM, SMEM, VMEM],
        out_specs=[VMEM] * (1 + NX),
        name="scale",
    )(lr_plan, ckpt_step, grads)


def copy_all(moves, sem):
    copies = [pltpu.make_async_copy(src, dst, sem.at[i]) for i, (src, dst) in enumerate(moves)]
    for copy in copies:
        copy.start()
    return copies


def cost(flops, bytes_accessed):
    return pl.CostEstimate(flops=flops, bytes_accessed=bytes_accessed, transcendentals=0)


def vmem_out(*shape, dtype=jnp.bfloat16):
    return jax.ShapeDtypeStruct(shape, dtype)


PARAMS = pltpu.CompilerParams(vmem_limit_bytes=16 * 2**20)


def own_products(lefts, rights):
    rows, width = lefts[0].shape
    q, nd, nk = rows // NX, len(lefts), len(rights[0])

    def kernel(*refs):
        left_in, right_in = refs[:nd], refs[nd : nd + 2 * nk]
        left, right, acc, sem = refs[nd + 2 * nk :]
        moves = [(left_in[i], left.at[i]) for i in range(nd)]
        moves += [
            (right_in[i], right.at[i // nk, :, pl.ds(i % nk * width, width)]) for i in range(2 * nk)
        ]
        copies = copy_all(moves, sem)
        for copy in copies[:nd]:
            copy.wait()
        for half in range(2):
            total = 0.0
            for k in range(nk):
                copies[nd + half * nk + k].wait()
                part = left[:, k * q : (k + 1) * q, :].reshape(nd * q, width)
                total = total + dot_t(part, right[half, :, k * width : (k + 1) * width])
            acc[half] = total

    return pl.pallas_call(
        kernel,
        out_shape=[
            vmem_out(nd, rows, width),
            vmem_out(2, rows, nk * width),
            vmem_out(2, nd * q, rows, dtype=jnp.float32),
        ],
        in_specs=[HBM] * (nd + 2 * nk),
        out_specs=[VMEM] * 3,
        scratch_shapes=[pltpu.SemaphoreType.DMA((nd + 2 * nk,))],
        compiler_params=PARAMS,
        cost_estimate=cost(4 * nd * q * rows * nk * width, 2 * (nd + 2 * nk) * rows * width),
        name="own",
    )(*lefts, *rights[0], *rights[1])


def all_products(left, acc, rights, fars):
    nd, rows, width = left.shape
    q, nk = rows // NX, len(rights[0])

    def kernel(left, acc, *refs):
        right_in, far_in = refs[: 2 * nk], refs[2 * nk : 2 * nk + 2]
        right, far, out, sem = refs[2 * nk + 2 :]
        moves = [
            (right_in[i], right.at[i // nk, :, pl.ds(i % nk * width, width)]) for i in range(2 * nk)
        ]
        moves += [(far_in[i], far.at[i]) for i in range(2)]
        copies = copy_all(moves, sem)

        def part(k):
            return left[:, k * q : (k + 1) * q, :].reshape(nd * q, width)

        for half in range(2):
            total = 0.0
            for k in range(nk):
                copies[half * nk + k].wait()
                total = total + dot_t(part(k), right[half, :, k * width : (k + 1) * width])
            out[2 * half + 1] = total.astype(jnp.bfloat16).reshape(nd, q, rows)
        for half in range(2):
            copies[2 * nk + half].wait()
            total = acc[half] + dot_t(part(nk - 1), far[half])
            out[2 * half] = total.astype(jnp.bfloat16).reshape(nd, q, rows)

    return pl.pallas_call(
        kernel,
        out_shape=[
            vmem_out(2, rows, nk * width),
            vmem_out(2, rows, width),
            vmem_out(4, nd, q, rows),
        ],
        in_specs=[VMEM, VMEM] + [HBM] * (2 * nk + 2),
        out_specs=[VMEM] * 3,
        scratch_shapes=[pltpu.SemaphoreType.DMA((2 * nk + 2,))],
        compiler_params=PARAMS,
        cost_estimate=cost(4 * nd * q * rows * (nk + 1) * width, 4 * (nk + 1) * rows * width),
        name="rest",
    )(left, acc, *rights[0], *rights[1], *fars)


def late_products(done, right_own, far_own, right_other, lefts, last, ds):
    nd, q, rows = done.shape[1:]
    width = far_own.shape[2]
    nl, half_rows, nk = len(lefts) + 1, rows // 2, NX

    def kernel(done, right_own, far_own, right_other, *refs):
        left_in, out, left, sem = refs[: nl + 1], refs[-3], refs[-2], refs[-1]
        z, a, c = (lax.axis_index(n) for n in (Z, YL, C))
        moves = [(left_in[i], left.at[i]) for i in range(nl - 1)]
        moves += [
            (left_in[nl - 1 + i], left.at[nl - 1, pl.ds(i * half_rows, half_rows)]) for i in range(2)
        ]
        copies = copy_all(moves, sem)

        def place(block, d):
            ylo, core = (a + block // 2) % 2, (c + block % 2) % 2
            return (ylo * 2 + core) * NZ + (z + d + NZ) % NZ

        for block in range(4):
            for i in range(nd):
                out[place(block, ds[i])] = done[block, i]
        for copy in copies:
            copy.wait()
        for block in range(4):
            half, total = block // 2, 0.0
            for k in range(nk):
                columns = slice(k * width, (k + 1) * width)
                if block % 2:
                    right = right_other[half, :, columns]
                else:
                    right = right_own[half, :, columns] if k < nk - 1 else far_own[half]
                total = total + dot_t(left[:, k * q : (k + 1) * q, :].reshape(nl * q, width), right)
            total = total.astype(jnp.bfloat16)
            for i in range(nl):
                out[place(block, ds[nd + i])] = total[i * q : (i + 1) * q]

    return pl.pallas_call(
        kernel,
        out_shape=vmem_out(4 * NZ, q, rows),
        in_specs=[VMEM] * 4 + [HBM] * (nl + 1),
        out_specs=VMEM,
        scratch_shapes=[
            pltpu.VMEM((nl, rows, width), jnp.bfloat16),
            pltpu.SemaphoreType.DMA((nl + 1,)),
        ],
        compiler_params=PARAMS,
        cost_estimate=cost(8 * nl * q * rows * nk * width, 2 * nl * rows * width),
        name="late",
    )(done, right_own, far_own, right_other, *lefts, *last)


def after(values, done):
    return lax.optimization_barrier((tuple(values), tuple(done)))[0]


def on_device(grads, lr_plan, ckpt_step):
    s, *quarters = scale(grads, lr_plan, ckpt_step)
    rows = s.shape[0]
    swap = lambda v: take_from(v, C, 2, 1)

    heads = [take_from(v, X, NX, dx) for v, dx in zip(quarters[1:], (1, -1, 2))]
    other = take_from(s, YL, 2, 1)
    ring = {0: jnp.concatenate([quarters[0]] + heads, axis=0)}
    ring[1], ring[-1] = take_from(ring[0], Z, NZ, 1), take_from(ring[0], Z, NZ, -1)
    (ready,) = after((s,), heads)
    fs, bs = take_from(ready, X, NX, 1), take_from(ready, X, NX, -1)

    (up,), (down,) = after((ring[1],), (fs,)), after((ring[-1],), (bs,))
    ring[2], ring[-2] = take_from(up, Z, NZ, 1), take_from(down, Z, NZ, -1)
    (f_ready,), (b_ready,) = after((other,), (fs,)), after((other,), (bs,))
    fo, bo = take_from(f_ready, X, NX, 1), take_from(b_ready, X, NX, -1)

    (up,), (down,) = after((ring[2],), (fo,)), after((ring[-2],), (bo,))
    ring[3], ring[-3] = take_from(up, Z, NZ, 1), take_from(down, Z, NZ, -1)
    (f_ready,), (b_ready,) = after((fs,), (fo,)), (bo,)
    far_s, far_o = take_from(f_ready, X, NX, 1), take_from(b_ready, X, NX, -1)

    first = [ring[d] for d in (0, 1, -1, 2, -2)]
    left, right_own, acc = own_products(first, [[s, fs, bs], [other, fo, bo]])
    half = rows // 2
    (down,) = (ring[-3],)
    last = (take_from(ring[3][:half], Z, NZ, 1), take_from(down[half:], Z, NZ, -1))

    ready = after((s, fs, bs, other), (fs, bs))
    ready += after((fo, bo, far_s, far_o), (ring[3], ring[-3]))
    swapped = [swap(v) for v in ready]
    right_other, far_own, done = all_products(
        left,
        acc,
        [swapped[:3] + swapped[6:7], swapped[3:6] + swapped[7:]],
        [far_s, far_o],
    )
    send = late_products(
        done, right_own, far_own, right_other, [ring[3], ring[-3]], last, (0, 1, -1, 2, -2, 3, -3, 4)
    )
    got = lax.all_to_all(send, (YL, C, YH, X), 0, 0)
    q = rows // NX
    got = got.reshape(2, 2, 2, NX, q, rows).astype(jnp.float32)
    total = got[:, :, 0] + got[:, :, 1]
    return total.reshape(2 * 2 * NX * q, rows).T


def solution(mesh):
    fine = Mesh(mesh.devices.reshape(NZ, 2, 2, 2, NX), (Z, YL, C, YH, X))
    spec = P((Z, YL, C), (YH, X))
    return jax.shard_map(
        on_device, mesh=fine, in_specs=(spec, P(), P()), out_specs=spec, check_vma=False
    )
```

time: 106 us -> 101 us (0.953)
  waiting for transfers between devices: 25.1 us -> 21.7 us
  local copies, waits for them, and re-layouts: 5.15 us -> 3.33 us
  starting transfers between devices: 38.8 us -> 40.1 us
  other arithmetic: 1.49 us -> 0.41 us
    ppermute x24 -> x26, waiting for transfers between devices: 25.1 us -> 21.7 us  [take_from(): lax.ppermute(value, axis, [(i, (i - step) % size) for i in range(size)])]
    unnamed x13 -> x5, local copies, waits for them, and re-layouts: 3.83 us -> 1.97 us
    ppermute x24 -> x26, starting transfers between devices: 38.8 us -> 40.1 us  [take_from(): lax.ppermute(value, axis, [(i, (i - step) % size) for i in range(size)])]
    select_n x1 -> x0, other arithmetic: 1.1 us -> none  [on_device(): ends = jnp.where(c == 0, ring[3], ring[-3])]
    pallas_call x2 -> x3, Pallas kernels: 11.5 us -> 11.4 us  [the longest x1 5.07 us: all_products(): pl.pallas_call(kernel, out_shape=[vmem_out(2, rows, nk * width), vmem_out...]
  transfers between devices with their start and end apart: 25 -> 26, of which waited for: 8 -> 7; matrix products, arithmetic and copies ran while one was open for 2% -> 1% of each run, Pallas kernels for 6% -> 8%
where the time goes in v2:
time: 101 us
  starting transfers between devices  40.1 us (40%)
  waiting for transfers between devices  21.7 us (21%)
  blocking collectives  21.7 us (21%)
  Pallas kernels  13.6 us (13%)
  local copies, waits for them, and re-layouts  3.33 us (3%)
    ppermute x26, starting transfers between devices, take_from(): lax.ppermute(value, axis, [(i, (i - step) % size) for i in range(size)])  40.1 us
    all_to_all x1, blocking collectives, on_device(): got = lax.all_to_all(send, (YL, C, YH, X), 0, 0)  21.7 us
    ppermute x26, waiting for transfers between devices, take_from(): lax.ppermute(value, axis, [(i, (i - step) % size) for i in range(size)])  21.7 us
    pallas_call x1, Pallas kernels, all_products(): pl.pallas_call(kernel, out_shape=[vmem_out(2, rows, nk * width), vmem_out...  5.07 us
    pallas_call x1, Pallas kernels, own_products(): pl.pallas_call(kernel, out_shape=[vmem_out(nd, rows, width), vmem_out(2,...  3.19 us
    pallas_call x1, Pallas kernels, late_products(): pl.pallas_call(kernel, out_shape=vmem_out(4 * NZ, q, rows), in_specs=[VME...  3.15 us
    pallas_call x1, Pallas kernels, scale(): pl.pallas_call(scale_kernel, out_shape=[jax.ShapeDtypeStruct((rows, width...  2.18 us
  transfers between devices with their start and end apart: 26, of which 7 were waited for; matrix products, arithmetic and copies ran while one was open for 1% of the time, Pallas kernels for 8%

profile of v2, /device:TPU:1, one launch (start us, length us, event | category | flops | bytes accessed | tf_op | source)
XLA Modules:
  0.0 101.1 jit_solution(8710867385462349120)
XLA Ops:
  0.0 2.2 %scale.1 = (bf16[256,1024]{1,0:T(8,128)(2,1)}, bf16[64,1024]{1,0:T(8,128)(2,1)}, bf16[64,1024]{1,0:T(8,128)(2,1)}, bf16[64,1024]{1,0:T(8,128)(2,1)}, bf16[64,1024]{1,0:T(8,128)(2,1)}) custom-call(f32[64]{0:T(128)} %plan_ref.1, s32[4]{0:T(128)} %step_ref.1, bf16[256,1024]{1,0:T(8,128)(2,1)} %grads_ref.1), custom_call_target="tpu_custom_call" | custom-call | tf_op jit(solution)/shard_map/scale/pallas_call | solution.py:47
  2.2 3.3 %collective-permute-start = (bf16[64,1024]{1,0:T(8,128)(2,1)}, bf16[64,1024]{1,0:T(8,128)(2,1)S(1)}, u32[]{:S(2)}, u32[]{:S(2)}) collective-permute-start(bf16[64,1024]{1,0:T(8,128)(2,1)} %get-tuple-element.33), channel_id=1, source_target_pairs={{0,3},{1,0},{2,1},{3,2},{4,7},{5,4},{6,5},{7,6},{8,11},{9,8},{10,9... | collective-permute-start | bytes 393224 | tf_op jit(solution)/shard_map/ppermute | solution.py:20
  5.5 0.0 collective-permute-start.1
  5.5 1.7 %collective-permute-start.2 = (bf16[64,1024]{1,0:T(8,128)(2,1)}, bf16[64,1024]{1,0:T(8,128)(2,1)S(1)}, u32[]{:S(2)}, u32[]{:S(2)}) collective-permute-start(bf16[64,1024]{1,0:T(8,128)(2,1)} %get-tuple-element.35), channel_id=1, source_target_pairs={{0,2},{1,3},{2,0},{3,1},{4,6},{5,7},{6,4},{7,5},{8,10},{9,11},{10,... | collective-permute-start | bytes 393224 | tf_op jit(solution)/shard_map/ppermute | solution.py:20
  7.2 0.9 constant_dynamic-update-slice_fusion.3
  8.1 0.0 collective-permute-done
  8.1 4.7 %collective-permute-done.1 = bf16[64,1024]{1,0:T(8,128)(2,1)S(1)} collective-permute-done((bf16[64,1024]{1,0:T(8,128)(2,1)}, bf16[64,1024]{1,0:T(8,128)(2,1)S(1)}, u32[]{:S(2)}, u32[]{:S(2)}) %collective-permute-start.1) | collective-permute-done | bytes 131104 | tf_op jit(solution)/shard_map/ppermute | solution.py:20
  12.9 0.0 collective-permute-done.2
  12.9 0.8 collective-permute-start.5
  13.8 5.6 %collective-permute-start.3 = (bf16[256,1024]{1,0:T(8,128)(2,1)S(1)}, bf16[256,1024]{1,0:T(8,128)(2,1)S(1)}, u32[]{:S(2)}, u32[]{:S(2)}) collective-permute-start(bf16[256,1024]{1,0:T(8,128)(2,1)S(1)} %constant_dynamic-update-slice_fusion.refs_0_), channel_id=1, source_target_pairs={{0,224},{32,0},{64,32},{96,64},{128,96},{160,128},{192,160},{224,1... | collective-permute-start | bytes 1572872 | tf_op jit(solution)/shard_map/ppermute | solution.py:20
  19.4 1.3 %collective-permute-start.9 = (bf16[256,1024]{1,0:T(8,128)(2,1)}, bf16[256,1024]{1,0:T(8,128)(2,1)S(1)}, u32[]{:S(2)}, u32[]{:S(2)}) collective-permute-start(bf16[256,1024]{1,0:T(8,128)(2,1)} %get-tuple-element.44.refs_5_), channel_id=1, source_target_pairs={{0,16},{16,0},{1,17},{17,1},{2,18},{18,2},{3,19},{19,3},{4,20},{20... | collective-permute-start | bytes 1572872 | tf_op jit(solution)/shard_map/ppermute | solution.py:20
  20.7 0.6 collective-permute-start.7
  21.3 0.0 collective-permute-start.4
  21.3 2.4 %collective-permute-done.5.refs_6_ = bf16[256,1024]{1,0:T(8,128)(2,1)S(1)} collective-permute-done((bf16[256,1024]{1,0:T(8,128)(2,1)}, bf16[256,1024]{1,0:T(8,128)(2,1)S(1)}, u32[]{:S(2)}, u32[]{:S(2)}) %collective-permute-start.5) | collective-permute-done | bytes 524320 | tf_op jit(solution)/shard_map/ppermute | solution.py:20
  23.7 4.2 %collective-permute-done.3.refs_1_ = bf16[256,1024]{1,0:T(8,128)(2,1)S(1)} collective-permute-done((bf16[256,1024]{1,0:T(8,128)(2,1)S(1)}, bf16[256,1024]{1,0:T(8,128)(2,1)S(1)}, u32[]{:S(2)}, u32[]{:S(2)}) %collective-permute-start.3) | collective-permute-done | bytes 524320 | tf_op jit(solution)/shard_map/ppermute | solution.py:20
  28.0 3.4 %collective-permute-start.6 = (bf16[256,1024]{1,0:T(8,128)(2,1)S(1)}, bf16[256,1024]{1,0:T(8,128)(2,1)S(1)}, u32[]{:S(2)}, u32[]{:S(2)}) collective-permute-start(bf16[256,1024]{1,0:T(8,128)(2,1)S(1)} %collective-permute-done.3.refs_1_), channel_id=1, source_target_pairs={{0,224},{32,0},{64,32},{96,64},{128,96},{160,128},{192,160},{224,1... | collective-permute-start | bytes 1572872 | tf_op jit(solution)/shard_map/ppermute | solution.py:20
  31.4 0.0 collective-permute-done.9.refs_8_
  31.4 1.9 %collective-permute-start.10 = (bf16[256,1024]{1,0:T(8,128)(2,1)S(1)}, bf16[256,1024]{1,0:T(8,128)(2,1)S(1)}, u32[]{:S(2)}, u32[]{:S(2)}) collective-permute-start(bf16[256,1024]{1,0:T(8,128)(2,1)S(1)} %collective-permute-done.9.refs_8_), channel_id=1, source_target_pairs={{0,3},{1,0},{2,1},{3,2},{4,7},{5,4},{6,5},{7,6},{8,11},{9,8},{10,9... | collective-permute-start | bytes 1572872 | tf_op jit(solution)/shard_map/ppermute | solution.py:20
  33.3 0.0 collective-permute-done.7.refs_7_
  33.3 0.0 collective-permute-done.4.refs_2_
  33.3 0.0 collective-permute-start.8
  33.3 0.1 collective-permute-start.11
  33.4 5.6 %collective-permute-done.6.refs_3_ = bf16[256,1024]{1,0:T(8,128)(2,1)S(1)} collective-permute-done((bf16[256,1024]{1,0:T(8,128)(2,1)S(1)}, bf16[256,1024]{1,0:T(8,128)(2,1)S(1)}, u32[]{:S(2)}, u32[]{:S(2)}) %collective-permute-start.6) | collective-permute-done | bytes 524320 | tf_op jit(solution)/shard_map/ppermute | solution.py:20
  39.0 2.6 %collective-permute-done.10.refs_9_ = bf16[256,1024]{1,0:T(8,128)(2,1)S(1)} collective-permute-done((bf16[256,1024]{1,0:T(8,128)(2,1)S(1)}, bf16[256,1024]{1,0:T(8,128)(2,1)S(1)}, u32[]{:S(2)}, u32[]{:S(2)}) %collective-permute-start.10) | collective-permute-done | bytes 524320 | tf_op jit(solution)/shard_map/ppermute | solution.py:20
  41.6 0.8 collective-permute-start.17
  42.4 2.0 %collective-permute-done.8.refs_4_ = bf16[256,1024]{1,0:T(8,128)(2,1)S(1)} collective-permute-done((bf16[256,1024]{1,0:T(8,128)(2,1)S(1)}, bf16[256,1024]{1,0:T(8,128)(2,1)S(1)}, u32[]{:S(2)}, u32[]{:S(2)}) %collective-permute-start.8) | collective-permute-done | bytes 524320 | tf_op jit(solution)/shard_map/ppermute | solution.py:20
  44.4 0.2 collective-permute-done.11.refs_10_
  44.6 0.0 collective-permute-start.18
  44.6 1.9 %collective-permute-start.15 = (bf16[256,1024]{1,0:T(8,128)(2,1)S(1)}, bf16[256,1024]{1,0:T(8,128)(2,1)S(1)}, u32[]{:S(2)}, u32[]{:S(2)}) collective-permute-start(bf16[256,1024]{1,0:T(8,128)(2,1)S(1)} %collective-permute-done.5.refs_6_), channel_id=1, source_target_pairs={{0,3},{1,0},{2,1},{3,2},{4,7},{5,4},{6,5},{7,6},{8,11},{9,8},{10,9... | collective-permute-start | bytes 1572872 | tf_op jit(solution)/shard_map/ppermute | solution.py:20
  46.5 0.0 collective-permute-start.16
  46.5 4.7 %collective-permute-start.12 = (bf16[256,1024]{1,0:T(8,128)(2,1)}, bf16[256,1024]{1,0:T(8,128)(2,1)S(1)}, u32[]{:S(2)}, u32[]{:S(2)}) collective-permute-start(bf16[256,1024]{1,0:T(8,128)(2,1)} %get-tuple-element.44.refs_5_), channel_id=1, source_target_pairs={{0,8},{8,0},{1,9},{9,1},{2,10},{10,2},{3,11},{11,3},{4,12},{12,4},... | collective-permute-start | bytes 1572872 | tf_op jit(solution)/shard_map/ppermute | solution.py:20
  51.2 0.0 collective-permute-done.17.refs_0_
  51.2 4.7 %collective-permute-start.13 = (bf16[256,1024]{1,0:T(8,128)(2,1)S(1)}, bf16[256,1024]{1,0:T(8,128)(2,1)S(1)}, u32[]{:S(2)}, u32[]{:S(2)}) collective-permute-start(bf16[256,1024]{1,0:T(8,128)(2,1)S(1)} %collective-permute-done.5.refs_6_), channel_id=1, source_target_pairs={{0,8},{8,0},{1,9},{9,1},{2,10},{10,2},{3,11},{11,3},{4,12},{12,4},... | collective-permute-start | bytes 1572872 | tf_op jit(solution)/shard_map/ppermute | solution.py:20
  55.9 0.0 collective-permute-done.18.refs_1_
  55.9 4.2 %collective-permute-start.14 = (bf16[256,1024]{1,0:T(8,128)(2,1)S(1)}, bf16[256,1024]{1,0:T(8,128)(2,1)S(1)}, u32[]{:S(2)}, u32[]{:S(2)}) collective-permute-start(bf16[256,1024]{1,0:T(8,128)(2,1)S(1)} %collective-permute-done.7.refs_7_), channel_id=1, source_target_pairs={{0,8},{8,0},{1,9},{9,1},{2,10},{10,2},{3,11},{11,3},{4,12},{12,4},... | collective-permute-start | bytes 1572872 | tf_op jit(solution)/shard_map/ppermute | solution.py:20
  60.1 0.0 collective-permute-done.15.refs_8_
  60.1 0.0 collective-permute-start.20
  60.1 0.0 collective-permute-done.16.refs_9_
  60.1 1.9 %collective-permute-start.19 = (bf16[256,1024]{1,0:T(8,128)(2,1)S(1)}, bf16[256,1024]{1,0:T(8,128)(2,1)S(1)}, u32[]{:S(2)}, u32[]{:S(2)}) collective-permute-start(bf16[256,1024]{1,0:T(8,128)(2,1)S(1)} %collective-permute-done.15.refs_8_), channel_id=1, source_target_pairs={{0,8},{8,0},{1,9},{9,1},{2,10},{10,2},{3,11},{11,3},{4,12},{12,4},... | collective-permute-start | bytes 1572872 | tf_op jit(solution)/shard_map/ppermute | solution.py:20
  62.0 0.0 collective-permute-done.12.refs_0_
  62.0 0.0 collective-permute-start.21
  62.0 0.0 collective-permute-done.13.refs_1_
  62.0 0.5 collective-permute-start.22
  62.5 0.0 collective-permute-done.14.refs_2_
  62.5 0.1 collective-permute-start.23
  62.7 0.0 collective-permute-done.20.refs_4_
  62.7 2.4 %collective-permute-start.24 = (bf16[128,1024]{1,0:T(8,128)(2,1)S(1)}, bf16[128,1024]{1,0:T(8,128)(2,1)S(1)}, u32[]{:S(2)}, u32[]{:S(2)}) collective-permute-start(bf16[128,1024]{1,0:T(8,128)(2,1)S(1)} %slice.16), channel_id=1, source_target_pairs={{0,224},{32,0},{64,32},{96,64},{128,96},{160,128},{192,160},{224,1... | collective-permute-start | bytes 786440 | tf_op jit(solution)/shard_map/ppermute | solution.py:20
  65.1 0.0 collective-permute-done.19.refs_3_
  65.1 0.0 collective-permute-start.25
  65.1 0.0 copy-start
  65.1 1.0 %copy-done = bf16[256,1024]{1,0:T(8,128)(2,1)S(1)} copy-done((bf16[256,1024]{1,0:T(8,128)(2,1)S(1)}, bf16[256,1024]{1,0:T(8,128)(2,1)}, u32[]{:S(2)}) %copy-start) | copy-done | bytes 524312
  66.1 3.2 %own.1 = (bf16[5,256,1024]{2,1,0:T(8,128)(2,1)S(1)}, bf16[2,256,3072]{2,1,0:T(8,128)(2,1)S(1)}, f32[2,320,256]{2,1,0:T(8,128)S(1)}) custom-call(bf16[256,1024]{1,0:T(8,128)(2,1)S(1)} %constant_dynamic-update-slice_fusion.refs_0_, bf16[256,1024]{1,0:T(8,128)(2,1)S(1)} %collective-permute-done.3.refs_1_, bf16[256,1024]{1,0:T(8,128)(2,1)S(1)} %collective-permute-done.4.refs_2_, ...), custom_call_target="tpu_custom_call" | custom-call | flops 1006632960 | bytes 5767168 | tf_op jit(solution)/shard_map/own/pallas_call | solution.py:96
  69.3 0.0 collective-permute-done.21.refs_5_
  69.3 0.0 collective-permute-done.22.refs_6_
  69.3 0.0 collective-permute-done.23.refs_7_
  69.3 5.1 %rest.1 = (bf16[2,256,4096]{2,1,0:T(8,128)(2,1)S(1)}, bf16[2,256,1024]{2,1,0:T(8,128)(2,1)S(1)}, bf16[4,5,64,256]{3,2,1,0:T(8,128)(2,1)S(1)}) custom-call(bf16[5,256,1024]{2,1,0:T(8,128)(2,1)S(1)} %get-tuple-element.42.left, f32[2,320,256]{2,1,0:T(8,128)S(1)} %get-tuple-element.43.acc, bf16[256,1024]{1,0:T(8,128)(2,1)S(1)} %collective-permute-done.12.refs_0_, ...), custom_call_target="tpu_custom_call" | custom-call | flops 1677721600 | bytes 5242880 | tf_op jit(solution)/shard_map/rest/pallas_call | solution.py:139
  74.4 0.0 collective-permute-done.24.refs_2_
  74.4 0.0 collective-permute-done.25.refs_3_
  74.4 3.1 %late.1 = bf16[32,64,256]{2,1,0:T(8,128)(2,1)S(1)} custom-call(bf16[4,5,64,256]{3,2,1,0:T(8,128)(2,1)S(1)} %get-tuple-element.55.done, bf16[2,256,3072]{2,1,0:T(8,128)(2,1)S(1)} %get-tuple-element.56.right_own, bf16[2,256,1024]{2,1,0:T(8,128)(2,1)S(1)} %get-tuple-element.57.far_own, bf16[2,256,4096]{2,1,0:T(8,128)(2,1)S(1)} %get-tuple-element.58.right_other, ...), custom_call_target="tpu_custom_call" | custom-call | flops 1610612736 | bytes 1572864 | tf_op jit(solution)/shard_map/late/pallas_call | solution.py:191
  77.6 21.7 %all_to_all.5 = bf16[32,64,256]{2,1,0:T(8,128)(2,1)S(1)} all-to-all(bf16[32,64,256]{2,1,0:T(8,128)(2,1)S(1)} %late.1), channel_id=1, replica_groups=mesh['z'=8,'ylo'=2,'core'=2,'yhi'=2,'x'=4] {'ylo','core','yhi','x'}, dimensions={0} | all-to-all | bytes 2097152 | tf_op jit(solution)/shard_map/all_to_all | solution.py:250
  99.3 0.3 convert.1
  99.6 0.2 fusion
  99.7 1.3 %copy.7 = f32[256,1024]{1,0:T(8,128)} copy(f32[256,1024]{0,1:T(8,128)S(1)} %bitcast.14) | data formatting | bytes 2097152 | tf_op jit(solution)/shard_map/transpose | solution.py:254
  (5 shorter events, 0.1 us)
Async XLA Ops:
  2.2 6.0 %collective-permute-start = (bf16[64,1024]{1,0:T(8,128)(2,1)}, bf16[64,1024]{1,0:T(8,128)(2,1)S(1)}, u32[]{:S(2)}, u32[]{:S(2)}) collective-permute-start(bf16[64,1024]{1,0:T(8,128)(2,1)} %get-tuple-element.33), channel_id=1, source_target_pairs={{0,3},{1,0},{2,1},{3,2},{4,7},{5,4},{6,5},{7,6},{8,11},{9,8},{10,9... | collective-permute-start | bytes 393224 | tf_op jit(solution)/shard_map/ppermute | solution.py:20
  5.5 7.4 %collective-permute-start.1 = (bf16[64,1024]{1,0:T(8,128)(2,1)}, bf16[64,1024]{1,0:T(8,128)(2,1)S(1)}, u32[]{:S(2)}, u32[]{:S(2)}) collective-permute-start(bf16[64,1024]{1,0:T(8,128)(2,1)} %get-tuple-element.34), channel_id=1, source_target_pairs={{0,1},{1,2},{2,3},{3,0},{4,5},{5,6},{6,7},{7,4},{8,9},{9,10},{10,1... | collective-permute-start | bytes 393224 | tf_op jit(solution)/shard_map/ppermute | solution.py:20
  5.5 7.4 %collective-permute-start.2 = (bf16[64,1024]{1,0:T(8,128)(2,1)}, bf16[64,1024]{1,0:T(8,128)(2,1)S(1)}, u32[]{:S(2)}, u32[]{:S(2)}) collective-permute-start(bf16[64,1024]{1,0:T(8,128)(2,1)} %get-tuple-element.35), channel_id=1, source_target_pairs={{0,2},{1,3},{2,0},{3,1},{4,6},{5,7},{6,4},{7,5},{8,10},{9,11},{10,... | collective-permute-start | bytes 393224 | tf_op jit(solution)/shard_map/ppermute | solution.py:20
  12.9 10.9 %collective-permute-start.5 = (bf16[256,1024]{1,0:T(8,128)(2,1)}, bf16[256,1024]{1,0:T(8,128)(2,1)S(1)}, u32[]{:S(2)}, u32[]{:S(2)}) collective-permute-start(bf16[256,1024]{1,0:T(8,128)(2,1)} %get-tuple-element.44.refs_5_), channel_id=1, source_target_pairs={{0,3},{1,0},{2,1},{3,2},{4,7},{5,4},{6,5},{7,6},{8,11},{9,8},{10,9... | collective-permute-start | bytes 1572872 | tf_op jit(solution)/shard_map/ppermute | solution.py:20
  13.8 14.2 %collective-permute-start.3 = (bf16[256,1024]{1,0:T(8,128)(2,1)S(1)}, bf16[256,1024]{1,0:T(8,128)(2,1)S(1)}, u32[]{:S(2)}, u32[]{:S(2)}) collective-permute-start(bf16[256,1024]{1,0:T(8,128)(2,1)S(1)} %constant_dynamic-update-slice_fusion.refs_0_), channel_id=1, source_target_pairs={{0,224},{32,0},{64,32},{96,64},{128,96},{160,128},{192,160},{224,1... | collective-permute-start | bytes 1572872 | tf_op jit(solution)/shard_map/ppermute | solution.py:20
  19.4 12.0 %collective-permute-start.9 = (bf16[256,1024]{1,0:T(8,128)(2,1)}, bf16[256,1024]{1,0:T(8,128)(2,1)S(1)}, u32[]{:S(2)}, u32[]{:S(2)}) collective-permute-start(bf16[256,1024]{1,0:T(8,128)(2,1)} %get-tuple-element.44.refs_5_), channel_id=1, source_target_pairs={{0,16},{16,0},{1,17},{17,1},{2,18},{18,2},{3,19},{19,3},{4,20},{20... | collective-permute-start | bytes 1572872 | tf_op jit(solution)/shard_map/ppermute | solution.py:20
  20.7 12.6 %collective-permute-start.7 = (bf16[256,1024]{1,0:T(8,128)(2,1)}, bf16[256,1024]{1,0:T(8,128)(2,1)S(1)}, u32[]{:S(2)}, u32[]{:S(2)}) collective-permute-start(bf16[256,1024]{1,0:T(8,128)(2,1)} %get-tuple-element.44.refs_5_), channel_id=1, source_target_pairs={{0,1},{1,2},{2,3},{3,0},{4,5},{5,6},{6,7},{7,4},{8,9},{9,10},{10,1... | collective-permute-start | bytes 1572872 | tf_op jit(solution)/shard_map/ppermute | solution.py:20
  21.3 12.0 %collective-permute-start.4 = (bf16[256,1024]{1,0:T(8,128)(2,1)S(1)}, bf16[256,1024]{1,0:T(8,128)(2,1)S(1)}, u32[]{:S(2)}, u32[]{:S(2)}) collective-permute-start(bf16[256,1024]{1,0:T(8,128)(2,1)S(1)} %constant_dynamic-update-slice_fusion.refs_0_), channel_id=1, source_target_pairs={{0,32},{32,64},{64,96},{96,128},{128,160},{160,192},{192,224},{224... | collective-permute-start | bytes 1572872 | tf_op jit(solution)/shard_map/ppermute | solution.py:20
  28.0 11.0 %collective-permute-start.6 = (bf16[256,1024]{1,0:T(8,128)(2,1)S(1)}, bf16[256,1024]{1,0:T(8,128)(2,1)S(1)}, u32[]{:S(2)}, u32[]{:S(2)}) collective-permute-start(bf16[256,1024]{1,0:T(8,128)(2,1)S(1)} %collective-permute-done.3.refs_1_), channel_id=1, source_target_pairs={{0,224},{32,0},{64,32},{96,64},{128,96},{160,128},{192,160},{224,1... | collective-permute-start | bytes 1572872 | tf_op jit(solution)/shard_map/ppermute | solution.py:20
  31.4 10.2 %collective-permute-start.10 = (bf16[256,1024]{1,0:T(8,128)(2,1)S(1)}, bf16[256,1024]{1,0:T(8,128)(2,1)S(1)}, u32[]{:S(2)}, u32[]{:S(2)}) collective-permute-start(bf16[256,1024]{1,0:T(8,128)(2,1)S(1)} %collective-permute-done.9.refs_8_), channel_id=1, source_target_pairs={{0,3},{1,0},{2,1},{3,2},{4,7},{5,4},{6,5},{7,6},{8,11},{9,8},{10,9... | collective-permute-start | bytes 1572872 | tf_op jit(solution)/shard_map/ppermute | solution.py:20
  33.3 11.1 %collective-permute-start.8 = (bf16[256,1024]{1,0:T(8,128)(2,1)S(1)}, bf16[256,1024]{1,0:T(8,128)(2,1)S(1)}, u32[]{:S(2)}, u32[]{:S(2)}) collective-permute-start(bf16[256,1024]{1,0:T(8,128)(2,1)S(1)} %collective-permute-done.4.refs_2_), channel_id=1, source_target_pairs={{0,32},{32,64},{64,96},{96,128},{128,160},{160,192},{192,224},{224... | collective-permute-start | bytes 1572872 | tf_op jit(solution)/shard_map/ppermute | solution.py:20
  33.3 11.2 %collective-permute-start.11 = (bf16[256,1024]{1,0:T(8,128)(2,1)S(1)}, bf16[256,1024]{1,0:T(8,128)(2,1)S(1)}, u32[]{:S(2)}, u32[]{:S(2)}) collective-permute-start(bf16[256,1024]{1,0:T(8,128)(2,1)S(1)} %collective-permute-done.9.refs_8_), channel_id=1, source_target_pairs={{0,1},{1,2},{2,3},{3,0},{4,5},{5,6},{6,7},{7,4},{8,9},{9,10},{10,1... | collective-permute-start | bytes 1572872 | tf_op jit(solution)/shard_map/ppermute | solution.py:20
  41.6 9.6 %collective-permute-start.17 = (bf16[256,1024]{1,0:T(8,128)(2,1)S(1)}, bf16[256,1024]{1,0:T(8,128)(2,1)S(1)}, u32[]{:S(2)}, u32[]{:S(2)}) collective-permute-start(bf16[256,1024]{1,0:T(8,128)(2,1)S(1)} %collective-permute-done.6.refs_3_), channel_id=1, source_target_pairs={{0,224},{32,0},{64,32},{96,64},{128,96},{160,128},{192,160},{224,1... | collective-permute-start | bytes 1572872 | tf_op jit(solution)/shard_map/ppermute | solution.py:20
  44.6 11.4 %collective-permute-start.18 = (bf16[256,1024]{1,0:T(8,128)(2,1)S(1)}, bf16[256,1024]{1,0:T(8,128)(2,1)S(1)}, u32[]{:S(2)}, u32[]{:S(2)}) collective-permute-start(bf16[256,1024]{1,0:T(8,128)(2,1)S(1)} %collective-permute-done.8.refs_4_), channel_id=1, source_target_pairs={{0,32},{32,64},{64,96},{96,128},{128,160},{160,192},{192,224},{224... | collective-permute-start | bytes 1572872 | tf_op jit(solution)/shard_map/ppermute | solution.py:20
  44.6 15.6 %collective-permute-start.15 = (bf16[256,1024]{1,0:T(8,128)(2,1)S(1)}, bf16[256,1024]{1,0:T(8,128)(2,1)S(1)}, u32[]{:S(2)}, u32[]{:S(2)}) collective-permute-start(bf16[256,1024]{1,0:T(8,128)(2,1)S(1)} %collective-permute-done.5.refs_6_), channel_id=1, source_target_pairs={{0,3},{1,0},{2,1},{3,2},{4,7},{5,4},{6,5},{7,6},{8,11},{9,8},{10,9... | collective-permute-start | bytes 1572872 | tf_op jit(solution)/shard_map/ppermute | solution.py:20
  46.5 13.7 %collective-permute-start.16 = (bf16[256,1024]{1,0:T(8,128)(2,1)S(1)}, bf16[256,1024]{1,0:T(8,128)(2,1)S(1)}, u32[]{:S(2)}, u32[]{:S(2)}) collective-permute-start(bf16[256,1024]{1,0:T(8,128)(2,1)S(1)} %collective-permute-done.11.refs_10_), channel_id=1, source_target_pairs={{0,1},{1,2},{2,3},{3,0},{4,5},{5,6},{6,7},{7,4},{8,9},{9,10},{10,1... | collective-permute-start | bytes 1572872 | tf_op jit(solution)/shard_map/ppermute | solution.py:20
  46.5 15.6 %collective-permute-start.12 = (bf16[256,1024]{1,0:T(8,128)(2,1)}, bf16[256,1024]{1,0:T(8,128)(2,1)S(1)}, u32[]{:S(2)}, u32[]{:S(2)}) collective-permute-start(bf16[256,1024]{1,0:T(8,128)(2,1)} %get-tuple-element.44.refs_5_), channel_id=1, source_target_pairs={{0,8},{8,0},{1,9},{9,1},{2,10},{10,2},{3,11},{11,3},{4,12},{12,4},... | collective-permute-start | bytes 1572872 | tf_op jit(solution)/shard_map/ppermute | solution.py:20
  51.2 10.8 %collective-permute-start.13 = (bf16[256,1024]{1,0:T(8,128)(2,1)S(1)}, bf16[256,1024]{1,0:T(8,128)(2,1)S(1)}, u32[]{:S(2)}, u32[]{:S(2)}) collective-permute-start(bf16[256,1024]{1,0:T(8,128)(2,1)S(1)} %collective-permute-done.5.refs_6_), channel_id=1, source_target_pairs={{0,8},{8,0},{1,9},{9,1},{2,10},{10,2},{3,11},{11,3},{4,12},{12,4},... | collective-permute-start | bytes 1572872 | tf_op jit(solution)/shard_map/ppermute | solution.py:20
  55.9 6.6 %collective-permute-start.14 = (bf16[256,1024]{1,0:T(8,128)(2,1)S(1)}, bf16[256,1024]{1,0:T(8,128)(2,1)S(1)}, u32[]{:S(2)}, u32[]{:S(2)}) collective-permute-start(bf16[256,1024]{1,0:T(8,128)(2,1)S(1)} %collective-permute-done.7.refs_7_), channel_id=1, source_target_pairs={{0,8},{8,0},{1,9},{9,1},{2,10},{10,2},{3,11},{11,3},{4,12},{12,4},... | collective-permute-start | bytes 1572872 | tf_op jit(solution)/shard_map/ppermute | solution.py:20
  60.1 2.6 %collective-permute-start.20 = (bf16[256,1024]{1,0:T(8,128)(2,1)S(1)}, bf16[256,1024]{1,0:T(8,128)(2,1)S(1)}, u32[]{:S(2)}, u32[]{:S(2)}) collective-permute-start(bf16[256,1024]{1,0:T(8,128)(2,1)S(1)} %collective-permute-done.9.refs_8_), channel_id=1, source_target_pairs={{0,8},{8,0},{1,9},{9,1},{2,10},{10,2},{3,11},{11,3},{4,12},{12,4},... | collective-permute-start | bytes 1572872 | tf_op jit(solution)/shard_map/ppermute | solution.py:20
  60.1 4.9 %collective-permute-start.19 = (bf16[256,1024]{1,0:T(8,128)(2,1)S(1)}, bf16[256,1024]{1,0:T(8,128)(2,1)S(1)}, u32[]{:S(2)}, u32[]{:S(2)}) collective-permute-start(bf16[256,1024]{1,0:T(8,128)(2,1)S(1)} %collective-permute-done.15.refs_8_), channel_id=1, source_target_pairs={{0,8},{8,0},{1,9},{9,1},{2,10},{10,2},{3,11},{11,3},{4,12},{12,4},... | collective-permute-start | bytes 1572872 | tf_op jit(solution)/shard_map/ppermute | solution.py:20
  62.0 7.3 %collective-permute-start.21 = (bf16[256,1024]{1,0:T(8,128)(2,1)S(1)}, bf16[256,1024]{1,0:T(8,128)(2,1)S(1)}, u32[]{:S(2)}, u32[]{:S(2)}) collective-permute-start(bf16[256,1024]{1,0:T(8,128)(2,1)S(1)} %collective-permute-done.10.refs_9_), channel_id=1, source_target_pairs={{0,8},{8,0},{1,9},{9,1},{2,10},{10,2},{3,11},{11,3},{4,12},{12,4},... | collective-permute-start | bytes 1572872 | tf_op jit(solution)/shard_map/ppermute | solution.py:20
  62.0 7.3 %collective-permute-start.22 = (bf16[256,1024]{1,0:T(8,128)(2,1)S(1)}, bf16[256,1024]{1,0:T(8,128)(2,1)S(1)}, u32[]{:S(2)}, u32[]{:S(2)}) collective-permute-start(bf16[256,1024]{1,0:T(8,128)(2,1)S(1)} %collective-permute-done.11.refs_10_), channel_id=1, source_target_pairs={{0,8},{8,0},{1,9},{9,1},{2,10},{10,2},{3,11},{11,3},{4,12},{12,4},... | collective-permute-start | bytes 1572872 | tf_op jit(solution)/shard_map/ppermute | solution.py:20
  62.5 6.8 %collective-permute-start.23 = (bf16[256,1024]{1,0:T(8,128)(2,1)S(1)}, bf16[256,1024]{1,0:T(8,128)(2,1)S(1)}, u32[]{:S(2)}, u32[]{:S(2)}) collective-permute-start(bf16[256,1024]{1,0:T(8,128)(2,1)S(1)} %collective-permute-done.16.refs_9_), channel_id=1, source_target_pairs={{0,8},{8,0},{1,9},{9,1},{2,10},{10,2},{3,11},{11,3},{4,12},{12,4},... | collective-permute-start | bytes 1572872 | tf_op jit(solution)/shard_map/ppermute | solution.py:20
  62.7 11.7 %collective-permute-start.24 = (bf16[128,1024]{1,0:T(8,128)(2,1)S(1)}, bf16[128,1024]{1,0:T(8,128)(2,1)S(1)}, u32[]{:S(2)}, u32[]{:S(2)}) collective-permute-start(bf16[128,1024]{1,0:T(8,128)(2,1)S(1)} %slice.16), channel_id=1, source_target_pairs={{0,224},{32,0},{64,32},{96,64},{128,96},{160,128},{192,160},{224,1... | collective-permute-start | bytes 786440 | tf_op jit(solution)/shard_map/ppermute | solution.py:20
  65.1 9.4 %collective-permute-start.25 = (bf16[128,1024]{1,0:T(8,128)(2,1)S(1)}, bf16[128,1024]{1,0:T(8,128)(2,1)S(1)}, u32[]{:S(2)}, u32[]{:S(2)}) collective-permute-start(bf16[128,1024]{1,0:T(8,128)(2,1)S(1)} %slice.17), channel_id=1, source_target_pairs={{0,32},{32,64},{64,96},{96,128},{128,160},{160,192},{192,224},{224... | collective-permute-start | bytes 786440 | tf_op jit(solution)/shard_map/ppermute | solution.py:20
  65.1 1.0 %copy-start = (bf16[256,1024]{1,0:T(8,128)(2,1)S(1)}, bf16[256,1024]{1,0:T(8,128)(2,1)}, u32[]{:S(2)}) copy-start(bf16[256,1024]{1,0:T(8,128)(2,1)} %get-tuple-element.44.refs_5_) | copy-start | bytes 1572868

commit v3 on v2

--- a/solution.py
+++ b/solution.py
@@ -235,7 +235,7 @@
     (down,) = (ring[-3],)
     last = (take_from(ring[3][:half], Z, NZ, 1), take_from(down[half:], Z, NZ, -1))
 
-    ready = after((s, fs, bs, other), (fs, bs))
+    ready = after((s,), (fs, bs)) + after((fs, bs, other), (acc,))
     ready += after((fo, bo, far_s, far_o), (ring[3], ring[-3]))
     swapped = [swap(v) for v in ready]
     right_other, far_own, done = all_products(

time: 101 us -> 101 us (level)
  starting transfers between devices: 40.1 us -> 35.9 us
  waiting for transfers between devices: 21.7 us -> 24.9 us
    ppermute x26, starting transfers between devices: 40.1 us -> 35.9 us  [take_from(): lax.ppermute(value, axis, [(i, (i - step) % size) for i in range(size)])]
    ppermute x26, waiting for transfers between devices: 21.7 us -> 24.9 us  [take_from(): lax.ppermute(value, axis, [(i, (i - step) % size) for i in range(size)])]
  transfers between devices with their start and end apart: 26 -> 26, of which waited for: 7 -> 9; matrix products, arithmetic and copies ran while one was open for 1% -> 1% of each run, Pallas kernels for 8% -> 8%
where the time goes in v3:
time: 101 us
  starting transfers between devices  35.9 us (36%)
  waiting for transfers between devices  24.9 us (25%)
  blocking collectives  22.2 us (22%)
  Pallas kernels  13.6 us (13%)
  local copies, waits for them, and re-layouts  3.33 us (3%)
    ppermute x26, starting transfers between devices, take_from(): lax.ppermute(value, axis, [(i, (i - step) % size) for i in range(size)])  35.9 us
    ppermute x26, waiting for transfers between devices, take_from(): lax.ppermute(value, axis, [(i, (i - step) % size) for i in range(size)])  24.9 us
    all_to_all x1, blocking collectives, on_device(): got = lax.all_to_all(send, (YL, C, YH, X), 0, 0)  22.2 us
    pallas_call x1, Pallas kernels, all_products(): pl.pallas_call(kernel, out_shape=[vmem_out(2, rows, nk * width), vmem_out...  5.07 us
    pallas_call x1, Pallas kernels, own_products(): pl.pallas_call(kernel, out_shape=[vmem_out(nd, rows, width), vmem_out(2,...  3.19 us
    pallas_call x1, Pallas kernels, late_products(): pl.pallas_call(kernel, out_shape=vmem_out(4 * NZ, q, rows), in_specs=[VME...  3.13 us
    pallas_call x1, Pallas kernels, scale(): pl.pallas_call(scale_kernel, out_shape=[jax.ShapeDtypeStruct((rows, width...  2.18 us
  transfers between devices with their start and end apart: 26, of which 9 were waited for; matrix products, arithmetic and copies ran while one was open for 1% of the time, Pallas kernels for 8%

profile of v3, /device:TPU:1, one launch (start us, length us, event | category | flops | bytes accessed | tf_op | source)
XLA Modules:
  0.0 100.5 jit_solution(4741151514815328525)
XLA Ops:
  0.0 2.2 %scale.1 = (bf16[256,1024]{1,0:T(8,128)(2,1)}, bf16[64,1024]{1,0:T(8,128)(2,1)}, bf16[64,1024]{1,0:T(8,128)(2,1)}, bf16[64,1024]{1,0:T(8,128)(2,1)}, bf16[64,1024]{1,0:T(8,128)(2,1)}) custom-call(f32[64]{0:T(128)} %plan_ref.1, s32[4]{0:T(128)} %step_ref.1, bf16[256,1024]{1,0:T(8,128)(2,1)} %grads_ref.1), custom_call_target="tpu_custom_call" | custom-call | tf_op jit(solution)/shard_map/scale/pallas_call | solution.py:47
  2.2 3.3 %collective-permute-start = (bf16[64,1024]{1,0:T(8,128)(2,1)}, bf16[64,1024]{1,0:T(8,128)(2,1)S(1)}, u32[]{:S(2)}, u32[]{:S(2)}) collective-permute-start(bf16[64,1024]{1,0:T(8,128)(2,1)} %get-tuple-element.33), channel_id=1, source_target_pairs={{0,3},{1,0},{2,1},{3,2},{4,7},{5,4},{6,5},{7,6},{8,11},{9,8},{10,9... | collective-permute-start | bytes 393224 | tf_op jit(solution)/shard_map/ppermute | solution.py:20
  5.5 0.0 collective-permute-start.1
  5.5 1.7 %collective-permute-start.2 = (bf16[64,1024]{1,0:T(8,128)(2,1)}, bf16[64,1024]{1,0:T(8,128)(2,1)S(1)}, u32[]{:S(2)}, u32[]{:S(2)}) collective-permute-start(bf16[64,1024]{1,0:T(8,128)(2,1)} %get-tuple-element.35), channel_id=1, source_target_pairs={{0,2},{1,3},{2,0},{3,1},{4,6},{5,7},{6,4},{7,5},{8,10},{9,11},{10,... | collective-permute-start | bytes 393224 | tf_op jit(solution)/shard_map/ppermute | solution.py:20
  7.2 0.9 constant_dynamic-update-slice_fusion.3
  8.1 0.0 collective-permute-done
  8.1 4.7 %collective-permute-done.1 = bf16[64,1024]{1,0:T(8,128)(2,1)S(1)} collective-permute-done((bf16[64,1024]{1,0:T(8,128)(2,1)}, bf16[64,1024]{1,0:T(8,128)(2,1)S(1)}, u32[]{:S(2)}, u32[]{:S(2)}) %collective-permute-start.1) | collective-permute-done | bytes 131104 | tf_op jit(solution)/shard_map/ppermute | solution.py:20
  12.9 0.0 collective-permute-done.2
  12.9 0.8 collective-permute-start.5
  13.8 5.6 %collective-permute-start.3 = (bf16[256,1024]{1,0:T(8,128)(2,1)S(1)}, bf16[256,1024]{1,0:T(8,128)(2,1)S(1)}, u32[]{:S(2)}, u32[]{:S(2)}) collective-permute-start(bf16[256,1024]{1,0:T(8,128)(2,1)S(1)} %constant_dynamic-update-slice_fusion.refs_0_), channel_id=1, source_target_pairs={{0,224},{32,0},{64,32},{96,64},{128,96},{160,128},{192,160},{224,1... | collective-permute-start | bytes 1572872 | tf_op jit(solution)/shard_map/ppermute | solution.py:20
  19.4 1.3 %collective-permute-start.9 = (bf16[256,1024]{1,0:T(8,128)(2,1)}, bf16[256,1024]{1,0:T(8,128)(2,1)S(1)}, u32[]{:S(2)}, u32[]{:S(2)}) collective-permute-start(bf16[256,1024]{1,0:T(8,128)(2,1)} %get-tuple-element.44.refs_5_), channel_id=1, source_target_pairs={{0,16},{16,0},{1,17},{17,1},{2,18},{18,2},{3,19},{19,3},{4,20},{20... | collective-permute-start | bytes 1572872 | tf_op jit(solution)/shard_map/ppermute | solution.py:20
  20.7 0.6 collective-permute-start.7
  21.3 0.0 collective-permute-start.4
  21.3 2.4 %collective-permute-done.5.refs_6_ = bf16[256,1024]{1,0:T(8,128)(2,1)S(1)} collective-permute-done((bf16[256,1024]{1,0:T(8,128)(2,1)}, bf16[256,1024]{1,0:T(8,128)(2,1)S(1)}, u32[]{:S(2)}, u32[]{:S(2)}) %collective-permute-start.5) | collective-permute-done | bytes 524320 | tf_op jit(solution)/shard_map/ppermute | solution.py:20
  23.7 4.2 %collective-permute-done.3.refs_1_ = bf16[256,1024]{1,0:T(8,128)(2,1)S(1)} collective-permute-done((bf16[256,1024]{1,0:T(8,128)(2,1)S(1)}, bf16[256,1024]{1,0:T(8,128)(2,1)S(1)}, u32[]{:S(2)}, u32[]{:S(2)}) %collective-permute-start.3) | collective-permute-done | bytes 524320 | tf_op jit(solution)/shard_map/ppermute | solution.py:20
  28.0 3.4 %collective-permute-start.6 = (bf16[256,1024]{1,0:T(8,128)(2,1)S(1)}, bf16[256,1024]{1,0:T(8,128)(2,1)S(1)}, u32[]{:S(2)}, u32[]{:S(2)}) collective-permute-start(bf16[256,1024]{1,0:T(8,128)(2,1)S(1)} %collective-permute-done.3.refs_1_), channel_id=1, source_target_pairs={{0,224},{32,0},{64,32},{96,64},{128,96},{160,128},{192,160},{224,1... | collective-permute-start | bytes 1572872 | tf_op jit(solution)/shard_map/ppermute | solution.py:20
  31.4 0.0 collective-permute-done.9.refs_8_
  31.4 1.9 %collective-permute-start.10 = (bf16[256,1024]{1,0:T(8,128)(2,1)S(1)}, bf16[256,1024]{1,0:T(8,128)(2,1)S(1)}, u32[]{:S(2)}, u32[]{:S(2)}) collective-permute-start(bf16[256,1024]{1,0:T(8,128)(2,1)S(1)} %collective-permute-done.9.refs_8_), channel_id=1, source_target_pairs={{0,3},{1,0},{2,1},{3,2},{4,7},{5,4},{6,5},{7,6},{8,11},{9,8},{10,9... | collective-permute-start | bytes 1572872 | tf_op jit(solution)/shard_map/ppermute | solution.py:20
  33.3 0.0 collective-permute-done.7.refs_7_
  33.3 0.0 collective-permute-done.4.refs_2_
  33.3 0.0 collective-permute-start.8
  33.3 0.1 collective-permute-start.11
  33.4 5.6 %collective-permute-done.6.refs_3_ = bf16[256,1024]{1,0:T(8,128)(2,1)S(1)} collective-permute-done((bf16[256,1024]{1,0:T(8,128)(2,1)S(1)}, bf16[256,1024]{1,0:T(8,128)(2,1)S(1)}, u32[]{:S(2)}, u32[]{:S(2)}) %collective-permute-start.6) | collective-permute-done | bytes 524320 | tf_op jit(solution)/shard_map/ppermute | solution.py:20
  39.0 2.6 %collective-permute-done.10.refs_9_ = bf16[256,1024]{1,0:T(8,128)(2,1)S(1)} collective-permute-done((bf16[256,1024]{1,0:T(8,128)(2,1)S(1)}, bf16[256,1024]{1,0:T(8,128)(2,1)S(1)}, u32[]{:S(2)}, u32[]{:S(2)}) %collective-permute-start.10) | collective-permute-done | bytes 524320 | tf_op jit(solution)/shard_map/ppermute | solution.py:20
  41.6 0.8 collective-permute-start.17
  42.4 2.0 %collective-permute-done.8.refs_4_ = bf16[256,1024]{1,0:T(8,128)(2,1)S(1)} collective-permute-done((bf16[256,1024]{1,0:T(8,128)(2,1)S(1)}, bf16[256,1024]{1,0:T(8,128)(2,1)S(1)}, u32[]{:S(2)}, u32[]{:S(2)}) %collective-permute-start.8) | collective-permute-done | bytes 524320 | tf_op jit(solution)/shard_map/ppermute | solution.py:20
  44.4 0.2 collective-permute-done.11.refs_10_
  44.6 0.0 collective-permute-start.18
  44.6 1.9 %collective-permute-start.15 = (bf16[256,1024]{1,0:T(8,128)(2,1)S(1)}, bf16[256,1024]{1,0:T(8,128)(2,1)S(1)}, u32[]{:S(2)}, u32[]{:S(2)}) collective-permute-start(bf16[256,1024]{1,0:T(8,128)(2,1)S(1)} %collective-permute-done.5.refs_6_), channel_id=1, source_target_pairs={{0,3},{1,0},{2,1},{3,2},{4,7},{5,4},{6,5},{7,6},{8,11},{9,8},{10,9... | collective-permute-start | bytes 1572872 | tf_op jit(solution)/shard_map/ppermute | solution.py:20
  46.5 0.0 collective-permute-start.16
  46.5 4.7 %collective-permute-start.12 = (bf16[256,1024]{1,0:T(8,128)(2,1)}, bf16[256,1024]{1,0:T(8,128)(2,1)S(1)}, u32[]{:S(2)}, u32[]{:S(2)}) collective-permute-start(bf16[256,1024]{1,0:T(8,128)(2,1)} %get-tuple-element.44.refs_5_), channel_id=1, source_target_pairs={{0,8},{8,0},{1,9},{9,1},{2,10},{10,2},{3,11},{11,3},{4,12},{12,4},... | collective-permute-start | bytes 1572872 | tf_op jit(solution)/shard_map/ppermute | solution.py:20
  51.2 0.0 copy-start
  51.2 1.0 %copy-done = bf16[256,1024]{1,0:T(8,128)(2,1)S(1)} copy-done((bf16[256,1024]{1,0:T(8,128)(2,1)S(1)}, bf16[256,1024]{1,0:T(8,128)(2,1)}, u32[]{:S(2)}) %copy-start) | copy-done | bytes 524312
  52.2 3.2 %own.1 = (bf16[5,256,1024]{2,1,0:T(8,128)(2,1)S(1)}, bf16[2,256,3072]{2,1,0:T(8,128)(2,1)S(1)}, f32[2,320,256]{2,1,0:T(8,128)S(1)}) custom-call(bf16[256,1024]{1,0:T(8,128)(2,1)S(1)} %constant_dynamic-update-slice_fusion.refs_0_, bf16[256,1024]{1,0:T(8,128)(2,1)S(1)} %collective-permute-done.3.refs_1_, bf16[256,1024]{1,0:T(8,128)(2,1)S(1)} %collective-permute-done.4.refs_2_, ...), custom_call_target="tpu_custom_call" | custom-call | flops 1006632960 | bytes 5767168 | tf_op jit(solution)/shard_map/own/pallas_call | solution.py:96
  55.4 0.0 collective-permute-done.17.refs_0_
  55.4 0.5 collective-permute-start.13
  55.9 0.0 collective-permute-done.18.refs_1_
  55.9 4.2 %collective-permute-start.14 = (bf16[256,1024]{1,0:T(8,128)(2,1)S(1)}, bf16[256,1024]{1,0:T(8,128)(2,1)S(1)}, u32[]{:S(2)}, u32[]{:S(2)}) collective-permute-start(bf16[256,1024]{1,0:T(8,128)(2,1)S(1)} %collective-permute-done.7.refs_7_), channel_id=1, source_target_pairs={{0,8},{8,0},{1,9},{9,1},{2,10},{10,2},{3,11},{11,3},{4,12},{12,4},... | collective-permute-start | bytes 1572872 | tf_op jit(solution)/shard_map/ppermute | solution.py:20
  60.1 0.0 collective-permute-done.15.refs_8_
  60.1 0.0 collective-permute-start.20
  60.1 0.0 collective-permute-done.16.refs_9_
  60.1 1.9 %collective-permute-start.19 = (bf16[256,1024]{1,0:T(8,128)(2,1)S(1)}, bf16[256,1024]{1,0:T(8,128)(2,1)S(1)}, u32[]{:S(2)}, u32[]{:S(2)}) collective-permute-start(bf16[256,1024]{1,0:T(8,128)(2,1)S(1)} %collective-permute-done.15.refs_8_), channel_id=1, source_target_pairs={{0,8},{8,0},{1,9},{9,1},{2,10},{10,2},{3,11},{11,3},{4,12},{12,4},... | collective-permute-start | bytes 1572872 | tf_op jit(solution)/shard_map/ppermute | solution.py:20
  62.0 0.0 collective-permute-done.12.refs_0_
  62.0 0.0 collective-permute-start.21
  62.0 0.0 collective-permute-done.13.refs_1_
  62.0 0.5 collective-permute-start.22
  62.5 0.0 collective-permute-done.14.refs_2_
  62.5 0.1 collective-permute-start.23
  62.7 0.0 collective-permute-done.20.refs_4_
  62.7 2.4 %collective-permute-start.24 = (bf16[128,1024]{1,0:T(8,128)(2,1)S(1)}, bf16[128,1024]{1,0:T(8,128)(2,1)S(1)}, u32[]{:S(2)}, u32[]{:S(2)}) collective-permute-start(bf16[128,1024]{1,0:T(8,128)(2,1)S(1)} %slice.16), channel_id=1, source_target_pairs={{0,224},{32,0},{64,32},{96,64},{128,96},{160,128},{192,160},{224,1... | collective-permute-start | bytes 786440 | tf_op jit(solution)/shard_map/ppermute | solution.py:20
  65.1 0.0 collective-permute-done.19.refs_3_
  65.1 0.0 collective-permute-start.25
  65.1 0.0 collective-permute-done.21.refs_5_
  65.1 0.0 collective-permute-done.22.refs_6_
  65.1 0.7 collective-permute-done.23.refs_7_
  65.8 5.1 %rest.1 = (bf16[2,256,4096]{2,1,0:T(8,128)(2,1)S(1)}, bf16[2,256,1024]{2,1,0:T(8,128)(2,1)S(1)}, bf16[4,5,64,256]{3,2,1,0:T(8,128)(2,1)S(1)}) custom-call(bf16[5,256,1024]{2,1,0:T(8,128)(2,1)S(1)} %get-tuple-element.42.left, f32[2,320,256]{2,1,0:T(8,128)S(1)} %get-tuple-element.43.acc, bf16[256,1024]{1,0:T(8,128)(2,1)S(1)} %collective-permute-done.12.refs_0_, ...), custom_call_target="tpu_custom_call" | custom-call | flops 1677721600 | bytes 5242880 | tf_op jit(solution)/shard_map/rest/pallas_call | solution.py:139
  70.9 0.0 collective-permute-done.24.refs_2_
  70.9 2.5 %collective-permute-done.25.refs_3_ = bf16[128,1024]{1,0:T(8,128)(2,1)S(1)} collective-permute-done((bf16[128,1024]{1,0:T(8,128)(2,1)S(1)}, bf16[128,1024]{1,0:T(8,128)(2,1)S(1)}, u32[]{:S(2)}, u32[]{:S(2)}) %collective-permute-start.25) | collective-permute-done | bytes 262176 | tf_op jit(solution)/shard_map/ppermute | solution.py:20
  73.4 3.1 %late.1 = bf16[32,64,256]{2,1,0:T(8,128)(2,1)S(1)} custom-call(bf16[4,5,64,256]{3,2,1,0:T(8,128)(2,1)S(1)} %get-tuple-element.55.done, bf16[2,256,3072]{2,1,0:T(8,128)(2,1)S(1)} %get-tuple-element.56.right_own, bf16[2,256,1024]{2,1,0:T(8,128)(2,1)S(1)} %get-tuple-element.57.far_own, bf16[2,256,4096]{2,1,0:T(8,128)(2,1)S(1)} %get-tuple-element.58.right_other, ...), custom_call_target="tpu_custom_call" | custom-call | flops 1610612736 | bytes 1572864 | tf_op jit(solution)/shard_map/late/pallas_call | solution.py:191
  76.5 22.2 %all_to_all.5 = bf16[32,64,256]{2,1,0:T(8,128)(2,1)S(1)} all-to-all(bf16[32,64,256]{2,1,0:T(8,128)(2,1)S(1)} %late.1), channel_id=1, replica_groups=mesh['z'=8,'ylo'=2,'core'=2,'yhi'=2,'x'=4] {'ylo','core','yhi','x'}, dimensions={0} | all-to-all | bytes 2097152 | tf_op jit(solution)/shard_map/all_to_all | solution.py:250
  98.8 0.3 convert.1
  99.0 0.2 fusion
  99.2 1.3 %copy.7 = f32[256,1024]{1,0:T(8,128)} copy(f32[256,1024]{0,1:T(8,128)S(1)} %bitcast.14) | data formatting | bytes 2097152 | tf_op jit(solution)/shard_map/transpose | solution.py:254
  (5 shorter events, 0.1 us)
Async XLA Ops:
  2.2 6.0 %collective-permute-start = (bf16[64,1024]{1,0:T(8,128)(2,1)}, bf16[64,1024]{1,0:T(8,128)(2,1)S(1)}, u32[]{:S(2)}, u32[]{:S(2)}) collective-permute-start(bf16[64,1024]{1,0:T(8,128)(2,1)} %get-tuple-element.33), channel_id=1, source_target_pairs={{0,3},{1,0},{2,1},{3,2},{4,7},{5,4},{6,5},{7,6},{8,11},{9,8},{10,9... | collective-permute-start | bytes 393224 | tf_op jit(solution)/shard_map/ppermute | solution.py:20
  5.5 7.4 %collective-permute-start.1 = (bf16[64,1024]{1,0:T(8,128)(2,1)}, bf16[64,1024]{1,0:T(8,128)(2,1)S(1)}, u32[]{:S(2)}, u32[]{:S(2)}) collective-permute-start(bf16[64,1024]{1,0:T(8,128)(2,1)} %get-tuple-element.34), channel_id=1, source_target_pairs={{0,1},{1,2},{2,3},{3,0},{4,5},{5,6},{6,7},{7,4},{8,9},{9,10},{10,1... | collective-permute-start | bytes 393224 | tf_op jit(solution)/shard_map/ppermute | solution.py:20
  5.5 7.4 %collective-permute-start.2 = (bf16[64,1024]{1,0:T(8,128)(2,1)}, bf16[64,1024]{1,0:T(8,128)(2,1)S(1)}, u32[]{:S(2)}, u32[]{:S(2)}) collective-permute-start(bf16[64,1024]{1,0:T(8,128)(2,1)} %get-tuple-element.35), channel_id=1, source_target_pairs={{0,2},{1,3},{2,0},{3,1},{4,6},{5,7},{6,4},{7,5},{8,10},{9,11},{10,... | collective-permute-start | bytes 393224 | tf_op jit(solution)/shard_map/ppermute | solution.py:20
  12.9 10.9 %collective-permute-start.5 = (bf16[256,1024]{1,0:T(8,128)(2,1)}, bf16[256,1024]{1,0:T(8,128)(2,1)S(1)}, u32[]{:S(2)}, u32[]{:S(2)}) collective-permute-start(bf16[256,1024]{1,0:T(8,128)(2,1)} %get-tuple-element.44.refs_5_), channel_id=1, source_target_pairs={{0,3},{1,0},{2,1},{3,2},{4,7},{5,4},{6,5},{7,6},{8,11},{9,8},{10,9... | collective-permute-start | bytes 1572872 | tf_op jit(solution)/shard_map/ppermute | solution.py:20
  13.8 14.2 %collective-permute-start.3 = (bf16[256,1024]{1,0:T(8,128)(2,1)S(1)}, bf16[256,1024]{1,0:T(8,128)(2,1)S(1)}, u32[]{:S(2)}, u32[]{:S(2)}) collective-permute-start(bf16[256,1024]{1,0:T(8,128)(2,1)S(1)} %constant_dynamic-update-slice_fusion.refs_0_), channel_id=1, source_target_pairs={{0,224},{32,0},{64,32},{96,64},{128,96},{160,128},{192,160},{224,1... | collective-permute-start | bytes 1572872 | tf_op jit(solution)/shard_map/ppermute | solution.py:20
  19.4 12.0 %collective-permute-start.9 = (bf16[256,1024]{1,0:T(8,128)(2,1)}, bf16[256,1024]{1,0:T(8,128)(2,1)S(1)}, u32[]{:S(2)}, u32[]{:S(2)}) collective-permute-start(bf16[256,1024]{1,0:T(8,128)(2,1)} %get-tuple-element.44.refs_5_), channel_id=1, source_target_pairs={{0,16},{16,0},{1,17},{17,1},{2,18},{18,2},{3,19},{19,3},{4,20},{20... | collective-permute-start | bytes 1572872 | tf_op jit(solution)/shard_map/ppermute | solution.py:20
  20.7 12.6 %collective-permute-start.7 = (bf16[256,1024]{1,0:T(8,128)(2,1)}, bf16[256,1024]{1,0:T(8,128)(2,1)S(1)}, u32[]{:S(2)}, u32[]{:S(2)}) collective-permute-start(bf16[256,1024]{1,0:T(8,128)(2,1)} %get-tuple-element.44.refs_5_), channel_id=1, source_target_pairs={{0,1},{1,2},{2,3},{3,0},{4,5},{5,6},{6,7},{7,4},{8,9},{9,10},{10,1... | collective-permute-start | bytes 1572872 | tf_op jit(solution)/shard_map/ppermute | solution.py:20
  21.3 12.0 %collective-permute-start.4 = (bf16[256,1024]{1,0:T(8,128)(2,1)S(1)}, bf16[256,1024]{1,0:T(8,128)(2,1)S(1)}, u32[]{:S(2)}, u32[]{:S(2)}) collective-permute-start(bf16[256,1024]{1,0:T(8,128)(2,1)S(1)} %constant_dynamic-update-slice_fusion.refs_0_), channel_id=1, source_target_pairs={{0,32},{32,64},{64,96},{96,128},{128,160},{160,192},{192,224},{224... | collective-permute-start | bytes 1572872 | tf_op jit(solution)/shard_map/ppermute | solution.py:20
  28.0 11.0 %collective-permute-start.6 = (bf16[256,1024]{1,0:T(8,128)(2,1)S(1)}, bf16[256,1024]{1,0:T(8,128)(2,1)S(1)}, u32[]{:S(2)}, u32[]{:S(2)}) collective-permute-start(bf16[256,1024]{1,0:T(8,128)(2,1)S(1)} %collective-permute-done.3.refs_1_), channel_id=1, source_target_pairs={{0,224},{32,0},{64,32},{96,64},{128,96},{160,128},{192,160},{224,1... | collective-permute-start | bytes 1572872 | tf_op jit(solution)/shard_map/ppermute | solution.py:20
  31.4 10.2 %collective-permute-start.10 = (bf16[256,1024]{1,0:T(8,128)(2,1)S(1)}, bf16[256,1024]{1,0:T(8,128)(2,1)S(1)}, u32[]{:S(2)}, u32[]{:S(2)}) collective-permute-start(bf16[256,1024]{1,0:T(8,128)(2,1)S(1)} %collective-permute-done.9.refs_8_), channel_id=1, source_target_pairs={{0,3},{1,0},{2,1},{3,2},{4,7},{5,4},{6,5},{7,6},{8,11},{9,8},{10,9... | collective-permute-start | bytes 1572872 | tf_op jit(solution)/shard_map/ppermute | solution.py:20
  33.3 11.1 %collective-permute-start.8 = (bf16[256,1024]{1,0:T(8,128)(2,1)S(1)}, bf16[256,1024]{1,0:T(8,128)(2,1)S(1)}, u32[]{:S(2)}, u32[]{:S(2)}) collective-permute-start(bf16[256,1024]{1,0:T(8,128)(2,1)S(1)} %collective-permute-done.4.refs_2_), channel_id=1, source_target_pairs={{0,32},{32,64},{64,96},{96,128},{128,160},{160,192},{192,224},{224... | collective-permute-start | bytes 1572872 | tf_op jit(solution)/shard_map/ppermute | solution.py:20
  33.3 11.2 %collective-permute-start.11 = (bf16[256,1024]{1,0:T(8,128)(2,1)S(1)}, bf16[256,1024]{1,0:T(8,128)(2,1)S(1)}, u32[]{:S(2)}, u32[]{:S(2)}) collective-permute-start(bf16[256,1024]{1,0:T(8,128)(2,1)S(1)} %collective-permute-done.9.refs_8_), channel_id=1, source_target_pairs={{0,1},{1,2},{2,3},{3,0},{4,5},{5,6},{6,7},{7,4},{8,9},{9,10},{10,1... | collective-permute-start | bytes 1572872 | tf_op jit(solution)/shard_map/ppermute | solution.py:20
  41.6 13.9 %collective-permute-start.17 = (bf16[256,1024]{1,0:T(8,128)(2,1)S(1)}, bf16[256,1024]{1,0:T(8,128)(2,1)S(1)}, u32[]{:S(2)}, u32[]{:S(2)}) collective-permute-start(bf16[256,1024]{1,0:T(8,128)(2,1)S(1)} %collective-permute-done.6.refs_3_), channel_id=1, source_target_pairs={{0,224},{32,0},{64,32},{96,64},{128,96},{160,128},{192,160},{224,1... | collective-permute-start | bytes 1572872 | tf_op jit(solution)/shard_map/ppermute | solution.py:20
  44.6 11.4 %collective-permute-start.18 = (bf16[256,1024]{1,0:T(8,128)(2,1)S(1)}, bf16[256,1024]{1,0:T(8,128)(2,1)S(1)}, u32[]{:S(2)}, u32[]{:S(2)}) collective-permute-start(bf16[256,1024]{1,0:T(8,128)(2,1)S(1)} %collective-permute-done.8.refs_4_), channel_id=1, source_target_pairs={{0,32},{32,64},{64,96},{96,128},{128,160},{160,192},{192,224},{224... | collective-permute-start | bytes 1572872 | tf_op jit(solution)/shard_map/ppermute | solution.py:20
  44.6 15.6 %collective-permute-start.15 = (bf16[256,1024]{1,0:T(8,128)(2,1)S(1)}, bf16[256,1024]{1,0:T(8,128)(2,1)S(1)}, u32[]{:S(2)}, u32[]{:S(2)}) collective-permute-start(bf16[256,1024]{1,0:T(8,128)(2,1)S(1)} %collective-permute-done.5.refs_6_), channel_id=1, source_target_pairs={{0,3},{1,0},{2,1},{3,2},{4,7},{5,4},{6,5},{7,6},{8,11},{9,8},{10,9... | collective-permute-start | bytes 1572872 | tf_op jit(solution)/shard_map/ppermute | solution.py:20
  46.5 13.7 %collective-permute-start.16 = (bf16[256,1024]{1,0:T(8,128)(2,1)S(1)}, bf16[256,1024]{1,0:T(8,128)(2,1)S(1)}, u32[]{:S(2)}, u32[]{:S(2)}) collective-permute-start(bf16[256,1024]{1,0:T(8,128)(2,1)S(1)} %collective-permute-done.11.refs_10_), channel_id=1, source_target_pairs={{0,1},{1,2},{2,3},{3,0},{4,5},{5,6},{6,7},{7,4},{8,9},{9,10},{10,1... | collective-permute-start | bytes 1572872 | tf_op jit(solution)/shard_map/ppermute | solution.py:20
  46.5 15.6 %collective-permute-start.12 = (bf16[256,1024]{1,0:T(8,128)(2,1)}, bf16[256,1024]{1,0:T(8,128)(2,1)S(1)}, u32[]{:S(2)}, u32[]{:S(2)}) collective-permute-start(bf16[256,1024]{1,0:T(8,128)(2,1)} %get-tuple-element.44.refs_5_), channel_id=1, source_target_pairs={{0,8},{8,0},{1,9},{9,1},{2,10},{10,2},{3,11},{11,3},{4,12},{12,4},... | collective-permute-start | bytes 1572872 | tf_op jit(solution)/shard_map/ppermute | solution.py:20
  51.2 1.0 %copy-start = (bf16[256,1024]{1,0:T(8,128)(2,1)S(1)}, bf16[256,1024]{1,0:T(8,128)(2,1)}, u32[]{:S(2)}) copy-start(bf16[256,1024]{1,0:T(8,128)(2,1)} %get-tuple-element.44.refs_5_) | copy-start | bytes 1572868
  55.4 6.6 %collective-permute-start.13 = (bf16[256,1024]{1,0:T(8,128)(2,1)S(1)}, bf16[256,1024]{1,0:T(8,128)(2,1)S(1)}, u32[]{:S(2)}, u32[]{:S(2)}) collective-permute-start(bf16[256,1024]{1,0:T(8,128)(2,1)S(1)} %collective-permute-done.5.refs_6_), channel_id=1, source_target_pairs={{0,8},{8,0},{1,9},{9,1},{2,10},{10,2},{3,11},{11,3},{4,12},{12,4},... | collective-permute-start | bytes 1572872 | tf_op jit(solution)/shard_map/ppermute | solution.py:20
  55.9 6.6 %collective-permute-start.14 = (bf16[256,1024]{1,0:T(8,128)(2,1)S(1)}, bf16[256,1024]{1,0:T(8,128)(2,1)S(1)}, u32[]{:S(2)}, u32[]{:S(2)}) collective-permute-start(bf16[256,1024]{1,0:T(8,128)(2,1)S(1)} %collective-permute-done.7.refs_7_), channel_id=1, source_target_pairs={{0,8},{8,0},{1,9},{9,1},{2,10},{10,2},{3,11},{11,3},{4,12},{12,4},... | collective-permute-start | bytes 1572872 | tf_op jit(solution)/shard_map/ppermute | solution.py:20
  60.1 2.6 %collective-permute-start.20 = (bf16[256,1024]{1,0:T(8,128)(2,1)S(1)}, bf16[256,1024]{1,0:T(8,128)(2,1)S(1)}, u32[]{:S(2)}, u32[]{:S(2)}) collective-permute-start(bf16[256,1024]{1,0:T(8,128)(2,1)S(1)} %collective-permute-done.9.refs_8_), channel_id=1, source_target_pairs={{0,8},{8,0},{1,9},{9,1},{2,10},{10,2},{3,11},{11,3},{4,12},{12,4},... | collective-permute-start | bytes 1572872 | tf_op jit(solution)/shard_map/ppermute | solution.py:20
  60.1 4.9 %collective-permute-start.19 = (bf16[256,1024]{1,0:T(8,128)(2,1)S(1)}, bf16[256,1024]{1,0:T(8,128)(2,1)S(1)}, u32[]{:S(2)}, u32[]{:S(2)}) collective-permute-start(bf16[256,1024]{1,0:T(8,128)(2,1)S(1)} %collective-permute-done.15.refs_8_), channel_id=1, source_target_pairs={{0,8},{8,0},{1,9},{9,1},{2,10},{10,2},{3,11},{11,3},{4,12},{12,4},... | collective-permute-start | bytes 1572872 | tf_op jit(solution)/shard_map/ppermute | solution.py:20
  62.0 3.0 %collective-permute-start.21 = (bf16[256,1024]{1,0:T(8,128)(2,1)S(1)}, bf16[256,1024]{1,0:T(8,128)(2,1)S(1)}, u32[]{:S(2)}, u32[]{:S(2)}) collective-permute-start(bf16[256,1024]{1,0:T(8,128)(2,1)S(1)} %collective-permute-done.10.refs_9_), channel_id=1, source_target_pairs={{0,8},{8,0},{1,9},{9,1},{2,10},{10,2},{3,11},{11,3},{4,12},{12,4},... | collective-permute-start | bytes 1572872 | tf_op jit(solution)/shard_map/ppermute | solution.py:20
  62.0 3.0 %collective-permute-start.22 = (bf16[256,1024]{1,0:T(8,128)(2,1)S(1)}, bf16[256,1024]{1,0:T(8,128)(2,1)S(1)}, u32[]{:S(2)}, u32[]{:S(2)}) collective-permute-start(bf16[256,1024]{1,0:T(8,128)(2,1)S(1)} %collective-permute-done.11.refs_10_), channel_id=1, source_target_pairs={{0,8},{8,0},{1,9},{9,1},{2,10},{10,2},{3,11},{11,3},{4,12},{12,4},... | collective-permute-start | bytes 1572872 | tf_op jit(solution)/shard_map/ppermute | solution.py:20
  62.5 3.3 %collective-permute-start.23 = (bf16[256,1024]{1,0:T(8,128)(2,1)S(1)}, bf16[256,1024]{1,0:T(8,128)(2,1)S(1)}, u32[]{:S(2)}, u32[]{:S(2)}) collective-permute-start(bf16[256,1024]{1,0:T(8,128)(2,1)S(1)} %collective-permute-done.16.refs_9_), channel_id=1, source_target_pairs={{0,8},{8,0},{1,9},{9,1},{2,10},{10,2},{3,11},{11,3},{4,12},{12,4},... | collective-permute-start | bytes 1572872 | tf_op jit(solution)/shard_map/ppermute | solution.py:20
  62.7 8.2 %collective-permute-start.24 = (bf16[128,1024]{1,0:T(8,128)(2,1)S(1)}, bf16[128,1024]{1,0:T(8,128)(2,1)S(1)}, u32[]{:S(2)}, u32[]{:S(2)}) collective-permute-start(bf16[128,1024]{1,0:T(8,128)(2,1)S(1)} %slice.16), channel_id=1, source_target_pairs={{0,224},{32,0},{64,32},{96,64},{128,96},{160,128},{192,160},{224,1... | collective-permute-start | bytes 786440 | tf_op jit(solution)/shard_map/ppermute | solution.py:20
  65.1 8.4 %collective-permute-start.25 = (bf16[128,1024]{1,0:T(8,128)(2,1)S(1)}, bf16[128,1024]{1,0:T(8,128)(2,1)S(1)}, u32[]{:S(2)}, u32[]{:S(2)}) collective-permute-start(bf16[128,1024]{1,0:T(8,128)(2,1)S(1)} %slice.17), channel_id=1, source_target_pairs={{0,32},{32,64},{64,96},{96,128},{128,160},{160,192},{192,224},{224... | collective-permute-start | bytes 786440 | tf_op jit(solution)/shard_map/ppermute | solution.py:20

commit v4 on v3

--- a/solution.py
+++ b/solution.py
@@ -155,14 +155,15 @@
 def late_products(done, right_own, far_own, right_other, lefts, last, ds):
     nd, q, rows = done.shape[1:]
     width = far_own.shape[2]
-    nl, half_rows, nk = len(lefts) + 1, rows // 2, NX
+    nl, cut, nk = len(lefts) + 1, last[0].shape[0], NX
 
     def kernel(done, right_own, far_own, right_other, *refs):
         left_in, out, left, sem = refs[: nl + 1], refs[-3], refs[-2], refs[-1]
         z, a, c = (lax.axis_index(n) for n in (Z, YL, C))
         moves = [(left_in[i], left.at[i]) for i in range(nl - 1)]
         moves += [
-            (left_in[nl - 1 + i], left.at[nl - 1, pl.ds(i * half_rows, half_rows)]) for i in range(2)
+            (left_in[nl - 1], left.at[nl - 1, pl.ds(0, cut)]),
+            (left_in[nl], left.at[nl - 1, pl.ds(cut, rows - cut)]),
         ]
         copies = copy_all(moves, sem)
 
@@ -231,9 +232,9 @@
 
     first = [ring[d] for d in (0, 1, -1, 2, -2)]
     left, right_own, acc = own_products(first, [[s, fs, bs], [other, fo, bo]])
-    half = rows // 2
+    cut = rows * 6 // 16
     (down,) = (ring[-3],)
-    last = (take_from(ring[3][:half], Z, NZ, 1), take_from(down[half:], Z, NZ, -1))
+    last = (take_from(ring[3][:cut], Z, NZ, 1), take_from(down[cut:], Z, NZ, -1))
 
     ready = after((s,), (fs, bs)) + after((fs, bs, other), (acc,))
     ready += after((fo, bo, far_s, far_o), (ring[3], ring[-3]))

time: 101 us -> 105 us (1.040)
  waiting for transfers between devices: 24.9 us -> 29.8 us
    ppermute x26, waiting for transfers between devices: 24.9 us -> 29.8 us  [take_from(): lax.ppermute(value, axis, [(i, (i - step) % size) for i in range(size)])]
  transfers between devices with their start and end apart: 26 -> 26, of which waited for: 9 -> 10; matrix products, arithmetic and copies ran while one was open for 1% -> 1% of each run, Pallas kernels for 8% -> 8%
where the time goes in v4:
time: 105 us
  starting transfers between devices  35.2 us (34%)
  waiting for transfers between devices  29.8 us (28%)
  blocking collectives  22.1 us (21%)
  Pallas kernels  13.9 us (13%)
  local copies, waits for them, and re-layouts  3.33 us (3%)
    ppermute x26, starting transfers between devices, take_from(): lax.ppermute(value, axis, [(i, (i - step) % size) for i in range(size)])  35.2 us
    ppermute x26, waiting for transfers between devices, take_from(): lax.ppermute(value, axis, [(i, (i - step) % size) for i in range(size)])  29.8 us
    all_to_all x1, blocking collectives, on_device(): got = lax.all_to_all(send, (YL, C, YH, X), 0, 0)  22.1 us
    pallas_call x1, Pallas kernels, all_products(): pl.pallas_call(kernel, out_shape=[vmem_out(2, rows, nk * width), vmem_out...  5.07 us
    pallas_call x1, Pallas kernels, late_products(): pl.pallas_call(kernel, out_shape=vmem_out(4 * NZ, q, rows), in_specs=[VME...  3.44 us
    pallas_call x1, Pallas kernels, own_products(): pl.pallas_call(kernel, out_shape=[vmem_out(nd, rows, width), vmem_out(2,...  3.2 us
    pallas_call x1, Pallas kernels, scale(): pl.pallas_call(scale_kernel, out_shape=[jax.ShapeDtypeStruct((rows, width...  2.18 us
  transfers between devices with their start and end apart: 26, of which 10 were waited for; matrix products, arithmetic and copies ran while one was open for 1% of the time, Pallas kernels for 8%

profile of v4, /device:TPU:1, one launch (start us, length us, event | category | flops | bytes accessed | tf_op | source)
XLA Modules:
  0.0 104.9 jit_solution(1988323720473843627)
XLA Ops:
  0.0 2.2 %scale.1 = (bf16[256,1024]{1,0:T(8,128)(2,1)}, bf16[64,1024]{1,0:T(8,128)(2,1)}, bf16[64,1024]{1,0:T(8,128)(2,1)}, bf16[64,1024]{1,0:T(8,128)(2,1)}, bf16[64,1024]{1,0:T(8,128)(2,1)}) custom-call(f32[64]{0:T(128)} %plan_ref.1, s32[4]{0:T(128)} %step_ref.1, bf16[256,1024]{1,0:T(8,128)(2,1)} %grads_ref.1), custom_call_target="tpu_custom_call" | custom-call | tf_op jit(solution)/shard_map/scale/pallas_call | solution.py:47
  2.2 3.3 %collective-permute-start = (bf16[64,1024]{1,0:T(8,128)(2,1)}, bf16[64,1024]{1,0:T(8,128)(2,1)S(1)}, u32[]{:S(2)}, u32[]{:S(2)}) collective-permute-start(bf16[64,1024]{1,0:T(8,128)(2,1)} %get-tuple-element.33), channel_id=1, source_target_pairs={{0,3},{1,0},{2,1},{3,2},{4,7},{5,4},{6,5},{7,6},{8,11},{9,8},{10,9... | collective-permute-start | bytes 393224 | tf_op jit(solution)/shard_map/ppermute | solution.py:20
  5.5 0.0 collective-permute-start.1
  5.5 1.7 %collective-permute-start.2 = (bf16[64,1024]{1,0:T(8,128)(2,1)}, bf16[64,1024]{1,0:T(8,128)(2,1)S(1)}, u32[]{:S(2)}, u32[]{:S(2)}) collective-permute-start(bf16[64,1024]{1,0:T(8,128)(2,1)} %get-tuple-element.35), channel_id=1, source_target_pairs={{0,2},{1,3},{2,0},{3,1},{4,6},{5,7},{6,4},{7,5},{8,10},{9,11},{10,... | collective-permute-start | bytes 393224 | tf_op jit(solution)/shard_map/ppermute | solution.py:20
  7.2 0.9 constant_dynamic-update-slice_fusion.3
  8.1 0.0 collective-permute-done
  8.1 4.7 %collective-permute-done.1 = bf16[64,1024]{1,0:T(8,128)(2,1)S(1)} collective-permute-done((bf16[64,1024]{1,0:T(8,128)(2,1)}, bf16[64,1024]{1,0:T(8,128)(2,1)S(1)}, u32[]{:S(2)}, u32[]{:S(2)}) %collective-permute-start.1) | collective-permute-done | bytes 131104 | tf_op jit(solution)/shard_map/ppermute | solution.py:20
  12.9 0.0 collective-permute-done.2
  12.9 0.8 collective-permute-start.5
  13.8 5.6 %collective-permute-start.3 = (bf16[256,1024]{1,0:T(8,128)(2,1)S(1)}, bf16[256,1024]{1,0:T(8,128)(2,1)S(1)}, u32[]{:S(2)}, u32[]{:S(2)}) collective-permute-start(bf16[256,1024]{1,0:T(8,128)(2,1)S(1)} %constant_dynamic-update-slice_fusion.refs_0_), channel_id=1, source_target_pairs={{0,224},{32,0},{64,32},{96,64},{128,96},{160,128},{192,160},{224,1... | collective-permute-start | bytes 1572872 | tf_op jit(solution)/shard_map/ppermute | solution.py:20
  19.4 1.3 %collective-permute-start.9 = (bf16[256,1024]{1,0:T(8,128)(2,1)}, bf16[256,1024]{1,0:T(8,128)(2,1)S(1)}, u32[]{:S(2)}, u32[]{:S(2)}) collective-permute-start(bf16[256,1024]{1,0:T(8,128)(2,1)} %get-tuple-element.44.refs_5_), channel_id=1, source_target_pairs={{0,16},{16,0},{1,17},{17,1},{2,18},{18,2},{3,19},{19,3},{4,20},{20... | collective-permute-start | bytes 1572872 | tf_op jit(solution)/shard_map/ppermute | solution.py:20
  20.7 0.6 collective-permute-start.7
  21.3 0.0 collective-permute-start.4
  21.3 2.4 %collective-permute-done.5.refs_6_ = bf16[256,1024]{1,0:T(8,128)(2,1)S(1)} collective-permute-done((bf16[256,1024]{1,0:T(8,128)(2,1)}, bf16[256,1024]{1,0:T(8,128)(2,1)S(1)}, u32[]{:S(2)}, u32[]{:S(2)}) %collective-permute-start.5) | collective-permute-done | bytes 524320 | tf_op jit(solution)/shard_map/ppermute | solution.py:20
  23.7 4.2 %collective-permute-done.3.refs_1_ = bf16[256,1024]{1,0:T(8,128)(2,1)S(1)} collective-permute-done((bf16[256,1024]{1,0:T(8,128)(2,1)S(1)}, bf16[256,1024]{1,0:T(8,128)(2,1)S(1)}, u32[]{:S(2)}, u32[]{:S(2)}) %collective-permute-start.3) | collective-permute-done | bytes 524320 | tf_op jit(solution)/shard_map/ppermute | solution.py:20
  28.0 3.4 %collective-permute-start.6 = (bf16[256,1024]{1,0:T(8,128)(2,1)S(1)}, bf16[256,1024]{1,0:T(8,128)(2,1)S(1)}, u32[]{:S(2)}, u32[]{:S(2)}) collective-permute-start(bf16[256,1024]{1,0:T(8,128)(2,1)S(1)} %collective-permute-done.3.refs_1_), channel_id=1, source_target_pairs={{0,224},{32,0},{64,32},{96,64},{128,96},{160,128},{192,160},{224,1... | collective-permute-start | bytes 1572872 | tf_op jit(solution)/shard_map/ppermute | solution.py:20
  31.4 0.0 collective-permute-done.9.refs_8_
  31.4 1.9 %collective-permute-start.10 = (bf16[256,1024]{1,0:T(8,128)(2,1)S(1)}, bf16[256,1024]{1,0:T(8,128)(2,1)S(1)}, u32[]{:S(2)}, u32[]{:S(2)}) collective-permute-start(bf16[256,1024]{1,0:T(8,128)(2,1)S(1)} %collective-permute-done.9.refs_8_), channel_id=1, source_target_pairs={{0,3},{1,0},{2,1},{3,2},{4,7},{5,4},{6,5},{7,6},{8,11},{9,8},{10,9... | collective-permute-start | bytes 1572872 | tf_op jit(solution)/shard_map/ppermute | solution.py:20
  33.3 0.0 collective-permute-done.7.refs_7_
  33.3 0.0 collective-permute-done.4.refs_2_
  33.3 0.0 collective-permute-start.8
  33.3 0.1 collective-permute-start.11
  33.4 5.6 %collective-permute-done.6.refs_3_ = bf16[256,1024]{1,0:T(8,128)(2,1)S(1)} collective-permute-done((bf16[256,1024]{1,0:T(8,128)(2,1)S(1)}, bf16[256,1024]{1,0:T(8,128)(2,1)S(1)}, u32[]{:S(2)}, u32[]{:S(2)}) %collective-permute-start.6) | collective-permute-done | bytes 524320 | tf_op jit(solution)/shard_map/ppermute | solution.py:20
  39.0 2.6 %collective-permute-done.10.refs_9_ = bf16[256,1024]{1,0:T(8,128)(2,1)S(1)} collective-permute-done((bf16[256,1024]{1,0:T(8,128)(2,1)S(1)}, bf16[256,1024]{1,0:T(8,128)(2,1)S(1)}, u32[]{:S(2)}, u32[]{:S(2)}) %collective-permute-start.10) | collective-permute-done | bytes 524320 | tf_op jit(solution)/shard_map/ppermute | solution.py:20
  41.6 0.8 collective-permute-start.17
  42.4 2.0 %collective-permute-done.8.refs_4_ = bf16[256,1024]{1,0:T(8,128)(2,1)S(1)} collective-permute-done((bf16[256,1024]{1,0:T(8,128)(2,1)S(1)}, bf16[256,1024]{1,0:T(8,128)(2,1)S(1)}, u32[]{:S(2)}, u32[]{:S(2)}) %collective-permute-start.8) | collective-permute-done | bytes 524320 | tf_op jit(solution)/shard_map/ppermute | solution.py:20
  44.4 0.2 collective-permute-done.11.refs_10_
  44.6 0.0 collective-permute-start.18
  44.6 1.9 %collective-permute-start.15 = (bf16[256,1024]{1,0:T(8,128)(2,1)S(1)}, bf16[256,1024]{1,0:T(8,128)(2,1)S(1)}, u32[]{:S(2)}, u32[]{:S(2)}) collective-permute-start(bf16[256,1024]{1,0:T(8,128)(2,1)S(1)} %collective-permute-done.5.refs_6_), channel_id=1, source_target_pairs={{0,3},{1,0},{2,1},{3,2},{4,7},{5,4},{6,5},{7,6},{8,11},{9,8},{10,9... | collective-permute-start | bytes 1572872 | tf_op jit(solution)/shard_map/ppermute | solution.py:20
  46.5 4.7 %collective-permute-start.12 = (bf16[256,1024]{1,0:T(8,128)(2,1)}, bf16[256,1024]{1,0:T(8,128)(2,1)S(1)}, u32[]{:S(2)}, u32[]{:S(2)}) collective-permute-start(bf16[256,1024]{1,0:T(8,128)(2,1)} %get-tuple-element.44.refs_5_), channel_id=1, source_target_pairs={{0,8},{8,0},{1,9},{9,1},{2,10},{10,2},{3,11},{11,3},{4,12},{12,4},... | collective-permute-start | bytes 1572872 | tf_op jit(solution)/shard_map/ppermute | solution.py:20
  51.2 0.0 collective-permute-start.16
  51.2 0.0 copy-start
  51.2 1.0 copy-done
  52.2 3.2 %own.1 = (bf16[5,256,1024]{2,1,0:T(8,128)(2,1)S(1)}, bf16[2,256,3072]{2,1,0:T(8,128)(2,1)S(1)}, f32[2,320,256]{2,1,0:T(8,128)S(1)}) custom-call(bf16[256,1024]{1,0:T(8,128)(2,1)S(1)} %constant_dynamic-update-slice_fusion.refs_0_, bf16[256,1024]{1,0:T(8,128)(2,1)S(1)} %collective-permute-done.3.refs_1_, bf16[256,1024]{1,0:T(8,128)(2,1)S(1)} %collective-permute-done.4.refs_2_, ...), custom_call_target="tpu_custom_call" | custom-call | flops 1006632960 | bytes 5767168 | tf_op jit(solution)/shard_map/own/pallas_call | solution.py:96
  55.4 0.0 collective-permute-done.17.refs_0_
  55.4 0.5 collective-permute-start.13
  55.9 0.0 collective-permute-done.18.refs_1_
  55.9 4.2 %collective-permute-start.14 = (bf16[256,1024]{1,0:T(8,128)(2,1)S(1)}, bf16[256,1024]{1,0:T(8,128)(2,1)S(1)}, u32[]{:S(2)}, u32[]{:S(2)}) collective-permute-start(bf16[256,1024]{1,0:T(8,128)(2,1)S(1)} %collective-permute-done.7.refs_7_), channel_id=1, source_target_pairs={{0,8},{8,0},{1,9},{9,1},{2,10},{10,2},{3,11},{11,3},{4,12},{12,4},... | collective-permute-start | bytes 1572872 | tf_op jit(solution)/shard_map/ppermute | solution.py:20
  60.1 0.0 collective-permute-done.15.refs_8_
  60.1 0.0 collective-permute-start.20
  60.1 5.8 %collective-permute-done.16.refs_9_ = bf16[256,1024]{1,0:T(8,128)(2,1)S(1)} collective-permute-done((bf16[256,1024]{1,0:T(8,128)(2,1)S(1)}, bf16[256,1024]{1,0:T(8,128)(2,1)S(1)}, u32[]{:S(2)}, u32[]{:S(2)}) %collective-permute-start.16) | collective-permute-done | bytes 524320 | tf_op jit(solution)/shard_map/ppermute | solution.py:20
  66.0 0.8 collective-permute-start.19
  66.7 0.0 collective-permute-done.12.refs_0_
  66.7 0.0 collective-permute-start.21
  66.7 0.0 collective-permute-done.13.refs_1_
  66.7 0.5 collective-permute-start.22
  67.3 0.0 collective-permute-done.14.refs_2_
  67.3 0.1 collective-permute-start.23
  67.4 0.0 collective-permute-done.20.refs_4_
  67.4 0.1 collective-permute-start.25
  67.5 0.8 collective-permute-done.19.refs_3_
  68.3 2.7 %collective-permute-start.24 = (bf16[96,1024]{1,0:T(8,128)(2,1)S(1)}, bf16[96,1024]{1,0:T(8,128)(2,1)S(1)}, u32[]{:S(2)}, u32[]{:S(2)}) collective-permute-start(bf16[96,1024]{1,0:T(8,128)(2,1)S(1)} %slice.16), channel_id=1, source_target_pairs={{0,224},{32,0},{64,32},{96,64},{128,96},{160,128},{192,160},{224,1... | collective-permute-start | bytes 589832 | tf_op jit(solution)/shard_map/ppermute | solution.py:20
  71.0 0.0 collective-permute-done.21.refs_5_
  71.0 0.0 collective-permute-done.22.refs_6_
  71.0 0.0 collective-permute-done.23.refs_7_
  71.0 5.1 %rest.1 = (bf16[2,256,4096]{2,1,0:T(8,128)(2,1)S(1)}, bf16[2,256,1024]{2,1,0:T(8,128)(2,1)S(1)}, bf16[4,5,64,256]{3,2,1,0:T(8,128)(2,1)S(1)}) custom-call(bf16[5,256,1024]{2,1,0:T(8,128)(2,1)S(1)} %get-tuple-element.42.left, f32[2,320,256]{2,1,0:T(8,128)S(1)} %get-tuple-element.43.acc, bf16[256,1024]{1,0:T(8,128)(2,1)S(1)} %collective-permute-done.12.refs_0_, ...), custom_call_target="tpu_custom_call" | custom-call | flops 1677721600 | bytes 5242880 | tf_op jit(solution)/shard_map/rest/pallas_call | solution.py:139
  76.1 0.0 collective-permute-done.24.refs_2_
  76.1 1.6 %collective-permute-done.25.refs_3_ = bf16[160,1024]{1,0:T(8,128)(2,1)S(1)} collective-permute-done((bf16[160,1024]{1,0:T(8,128)(2,1)S(1)}, bf16[160,1024]{1,0:T(8,128)(2,1)S(1)}, u32[]{:S(2)}, u32[]{:S(2)}) %collective-permute-start.25) | collective-permute-done | bytes 327712 | tf_op jit(solution)/shard_map/ppermute | solution.py:20
  77.7 3.4 %late.1 = bf16[32,64,256]{2,1,0:T(8,128)(2,1)S(1)} custom-call(bf16[4,5,64,256]{3,2,1,0:T(8,128)(2,1)S(1)} %get-tuple-element.55.done, bf16[2,256,3072]{2,1,0:T(8,128)(2,1)S(1)} %get-tuple-element.56.right_own, bf16[2,256,1024]{2,1,0:T(8,128)(2,1)S(1)} %get-tuple-element.57.far_own, bf16[2,256,4096]{2,1,0:T(8,128)(2,1)S(1)} %get-tuple-element.58.right_other, ...), custom_call_target="tpu_custom_call" | custom-call | flops 1610612736 | bytes 1572864 | tf_op jit(solution)/shard_map/late/pallas_call | solution.py:192
  81.1 22.1 %all_to_all.5 = bf16[32,64,256]{2,1,0:T(8,128)(2,1)S(1)} all-to-all(bf16[32,64,256]{2,1,0:T(8,128)(2,1)S(1)} %late.1), channel_id=1, replica_groups=mesh['z'=8,'ylo'=2,'core'=2,'yhi'=2,'x'=4] {'ylo','core','yhi','x'}, dimensions={0} | all-to-all | bytes 2097152 | tf_op jit(solution)/shard_map/all_to_all | solution.py:251
  103.2 0.3 convert.1
  103.5 0.2 fusion
  103.6 1.3 %copy.7 = f32[256,1024]{1,0:T(8,128)} copy(f32[256,1024]{0,1:T(8,128)S(1)} %bitcast.14) | data formatting | bytes 2097152 | tf_op jit(solution)/shard_map/transpose | solution.py:255
  (5 shorter events, 0.1 us)
Async XLA Ops:
  2.2 6.0 %collective-permute-start = (bf16[64,1024]{1,0:T(8,128)(2,1)}, bf16[64,1024]{1,0:T(8,128)(2,1)S(1)}, u32[]{:S(2)}, u32[]{:S(2)}) collective-permute-start(bf16[64,1024]{1,0:T(8,128)(2,1)} %get-tuple-element.33), channel_id=1, source_target_pairs={{0,3},{1,0},{2,1},{3,2},{4,7},{5,4},{6,5},{7,6},{8,11},{9,8},{10,9... | collective-permute-start | bytes 393224 | tf_op jit(solution)/shard_map/ppermute | solution.py:20
  5.5 7.4 %collective-permute-start.1 = (bf16[64,1024]{1,0:T(8,128)(2,1)}, bf16[64,1024]{1,0:T(8,128)(2,1)S(1)}, u32[]{:S(2)}, u32[]{:S(2)}) collective-permute-start(bf16[64,1024]{1,0:T(8,128)(2,1)} %get-tuple-element.34), channel_id=1, source_target_pairs={{0,1},{1,2},{2,3},{3,0},{4,5},{5,6},{6,7},{7,4},{8,9},{9,10},{10,1... | collective-permute-start | bytes 393224 | tf_op jit(solution)/shard_map/ppermute | solution.py:20
  5.5 7.4 %collective-permute-start.2 = (bf16[64,1024]{1,0:T(8,128)(2,1)}, bf16[64,1024]{1,0:T(8,128)(2,1)S(1)}, u32[]{:S(2)}, u32[]{:S(2)}) collective-permute-start(bf16[64,1024]{1,0:T(8,128)(2,1)} %get-tuple-element.35), channel_id=1, source_target_pairs={{0,2},{1,3},{2,0},{3,1},{4,6},{5,7},{6,4},{7,5},{8,10},{9,11},{10,... | collective-permute-start | bytes 393224 | tf_op jit(solution)/shard_map/ppermute | solution.py:20
  12.9 10.9 %collective-permute-start.5 = (bf16[256,1024]{1,0:T(8,128)(2,1)}, bf16[256,1024]{1,0:T(8,128)(2,1)S(1)}, u32[]{:S(2)}, u32[]{:S(2)}) collective-permute-start(bf16[256,1024]{1,0:T(8,128)(2,1)} %get-tuple-element.44.refs_5_), channel_id=1, source_target_pairs={{0,3},{1,0},{2,1},{3,2},{4,7},{5,4},{6,5},{7,6},{8,11},{9,8},{10,9... | collective-permute-start | bytes 1572872 | tf_op jit(solution)/shard_map/ppermute | solution.py:20
  13.8 14.2 %collective-permute-start.3 = (bf16[256,1024]{1,0:T(8,128)(2,1)S(1)}, bf16[256,1024]{1,0:T(8,128)(2,1)S(1)}, u32[]{:S(2)}, u32[]{:S(2)}) collective-permute-start(bf16[256,1024]{1,0:T(8,128)(2,1)S(1)} %constant_dynamic-update-slice_fusion.refs_0_), channel_id=1, source_target_pairs={{0,224},{32,0},{64,32},{96,64},{128,96},{160,128},{192,160},{224,1... | collective-permute-start | bytes 1572872 | tf_op jit(solution)/shard_map/ppermute | solution.py:20
  19.4 12.0 %collective-permute-start.9 = (bf16[256,1024]{1,0:T(8,128)(2,1)}, bf16[256,1024]{1,0:T(8,128)(2,1)S(1)}, u32[]{:S(2)}, u32[]{:S(2)}) collective-permute-start(bf16[256,1024]{1,0:T(8,128)(2,1)} %get-tuple-element.44.refs_5_), channel_id=1, source_target_pairs={{0,16},{16,0},{1,17},{17,1},{2,18},{18,2},{3,19},{19,3},{4,20},{20... | collective-permute-start | bytes 1572872 | tf_op jit(solution)/shard_map/ppermute | solution.py:20
  20.7 12.6 %collective-permute-start.7 = (bf16[256,1024]{1,0:T(8,128)(2,1)}, bf16[256,1024]{1,0:T(8,128)(2,1)S(1)}, u32[]{:S(2)}, u32[]{:S(2)}) collective-permute-start(bf16[256,1024]{1,0:T(8,128)(2,1)} %get-tuple-element.44.refs_5_), channel_id=1, source_target_pairs={{0,1},{1,2},{2,3},{3,0},{4,5},{5,6},{6,7},{7,4},{8,9},{9,10},{10,1... | collective-permute-start | bytes 1572872 | tf_op jit(solution)/shard_map/ppermute | solution.py:20
  21.3 12.0 %collective-permute-start.4 = (bf16[256,1024]{1,0:T(8,128)(2,1)S(1)}, bf16[256,1024]{1,0:T(8,128)(2,1)S(1)}, u32[]{:S(2)}, u32[]{:S(2)}) collective-permute-start(bf16[256,1024]{1,0:T(8,128)(2,1)S(1)} %constant_dynamic-update-slice_fusion.refs_0_), channel_id=1, source_target_pairs={{0,32},{32,64},{64,96},{96,128},{128,160},{160,192},{192,224},{224... | collective-permute-start | bytes 1572872 | tf_op jit(solution)/shard_map/ppermute | solution.py:20
  28.0 11.0 %collective-permute-start.6 = (bf16[256,1024]{1,0:T(8,128)(2,1)S(1)}, bf16[256,1024]{1,0:T(8,128)(2,1)S(1)}, u32[]{:S(2)}, u32[]{:S(2)}) collective-permute-start(bf16[256,1024]{1,0:T(8,128)(2,1)S(1)} %collective-permute-done.3.refs_1_), channel_id=1, source_target_pairs={{0,224},{32,0},{64,32},{96,64},{128,96},{160,128},{192,160},{224,1... | collective-permute-start | bytes 1572872 | tf_op jit(solution)/shard_map/ppermute | solution.py:20
  31.4 10.2 %collective-permute-start.10 = (bf16[256,1024]{1,0:T(8,128)(2,1)S(1)}, bf16[256,1024]{1,0:T(8,128)(2,1)S(1)}, u32[]{:S(2)}, u32[]{:S(2)}) collective-permute-start(bf16[256,1024]{1,0:T(8,128)(2,1)S(1)} %collective-permute-done.9.refs_8_), channel_id=1, source_target_pairs={{0,3},{1,0},{2,1},{3,2},{4,7},{5,4},{6,5},{7,6},{8,11},{9,8},{10,9... | collective-permute-start | bytes 1572872 | tf_op jit(solution)/shard_map/ppermute | solution.py:20
  33.3 11.1 %collective-permute-start.8 = (bf16[256,1024]{1,0:T(8,128)(2,1)S(1)}, bf16[256,1024]{1,0:T(8,128)(2,1)S(1)}, u32[]{:S(2)}, u32[]{:S(2)}) collective-permute-start(bf16[256,1024]{1,0:T(8,128)(2,1)S(1)} %collective-permute-done.4.refs_2_), channel_id=1, source_target_pairs={{0,32},{32,64},{64,96},{96,128},{128,160},{160,192},{192,224},{224... | collective-permute-start | bytes 1572872 | tf_op jit(solution)/shard_map/ppermute | solution.py:20
  33.3 11.2 %collective-permute-start.11 = (bf16[256,1024]{1,0:T(8,128)(2,1)S(1)}, bf16[256,1024]{1,0:T(8,128)(2,1)S(1)}, u32[]{:S(2)}, u32[]{:S(2)}) collective-permute-start(bf16[256,1024]{1,0:T(8,128)(2,1)S(1)} %collective-permute-done.9.refs_8_), channel_id=1, source_target_pairs={{0,1},{1,2},{2,3},{3,0},{4,5},{5,6},{6,7},{7,4},{8,9},{9,10},{10,1... | collective-permute-start | bytes 1572872 | tf_op jit(solution)/shard_map/ppermute | solution.py:20
  41.6 13.9 %collective-permute-start.17 = (bf16[256,1024]{1,0:T(8,128)(2,1)S(1)}, bf16[256,1024]{1,0:T(8,128)(2,1)S(1)}, u32[]{:S(2)}, u32[]{:S(2)}) collective-permute-start(bf16[256,1024]{1,0:T(8,128)(2,1)S(1)} %collective-permute-done.6.refs_3_), channel_id=1, source_target_pairs={{0,224},{32,0},{64,32},{96,64},{128,96},{160,128},{192,160},{224,1... | collective-permute-start | bytes 1572872 | tf_op jit(solution)/shard_map/ppermute | solution.py:20
  44.6 11.4 %collective-permute-start.18 = (bf16[256,1024]{1,0:T(8,128)(2,1)S(1)}, bf16[256,1024]{1,0:T(8,128)(2,1)S(1)}, u32[]{:S(2)}, u32[]{:S(2)}) collective-permute-start(bf16[256,1024]{1,0:T(8,128)(2,1)S(1)} %collective-permute-done.8.refs_4_), channel_id=1, source_target_pairs={{0,32},{32,64},{64,96},{96,128},{128,160},{160,192},{192,224},{224... | collective-permute-start | bytes 1572872 | tf_op jit(solution)/shard_map/ppermute | solution.py:20
  44.6 15.6 %collective-permute-start.15 = (bf16[256,1024]{1,0:T(8,128)(2,1)S(1)}, bf16[256,1024]{1,0:T(8,128)(2,1)S(1)}, u32[]{:S(2)}, u32[]{:S(2)}) collective-permute-start(bf16[256,1024]{1,0:T(8,128)(2,1)S(1)} %collective-permute-done.5.refs_6_), channel_id=1, source_target_pairs={{0,3},{1,0},{2,1},{3,2},{4,7},{5,4},{6,5},{7,6},{8,11},{9,8},{10,9... | collective-permute-start | bytes 1572872 | tf_op jit(solution)/shard_map/ppermute | solution.py:20
  46.5 20.3 %collective-permute-start.12 = (bf16[256,1024]{1,0:T(8,128)(2,1)}, bf16[256,1024]{1,0:T(8,128)(2,1)S(1)}, u32[]{:S(2)}, u32[]{:S(2)}) collective-permute-start(bf16[256,1024]{1,0:T(8,128)(2,1)} %get-tuple-element.44.refs_5_), channel_id=1, source_target_pairs={{0,8},{8,0},{1,9},{9,1},{2,10},{10,2},{3,11},{11,3},{4,12},{12,4},... | collective-permute-start | bytes 1572872 | tf_op jit(solution)/shard_map/ppermute | solution.py:20
  51.2 14.8 %collective-permute-start.16 = (bf16[256,1024]{1,0:T(8,128)(2,1)S(1)}, bf16[256,1024]{1,0:T(8,128)(2,1)S(1)}, u32[]{:S(2)}, u32[]{:S(2)}) collective-permute-start(bf16[256,1024]{1,0:T(8,128)(2,1)S(1)} %collective-permute-done.11.refs_10_), channel_id=1, source_target_pairs={{0,1},{1,2},{2,3},{3,0},{4,5},{5,6},{6,7},{7,4},{8,9},{9,10},{10,1... | collective-permute-start | bytes 1572872 | tf_op jit(solution)/shard_map/ppermute | solution.py:20
  51.2 1.0 copy-start
  55.4 11.3 %collective-permute-start.13 = (bf16[256,1024]{1,0:T(8,128)(2,1)S(1)}, bf16[256,1024]{1,0:T(8,128)(2,1)S(1)}, u32[]{:S(2)}, u32[]{:S(2)}) collective-permute-start(bf16[256,1024]{1,0:T(8,128)(2,1)S(1)} %collective-permute-done.5.refs_6_), channel_id=1, source_target_pairs={{0,8},{8,0},{1,9},{9,1},{2,10},{10,2},{3,11},{11,3},{4,12},{12,4},... | collective-permute-start | bytes 1572872 | tf_op jit(solution)/shard_map/ppermute | solution.py:20
  55.9 11.3 %collective-permute-start.14 = (bf16[256,1024]{1,0:T(8,128)(2,1)S(1)}, bf16[256,1024]{1,0:T(8,128)(2,1)S(1)}, u32[]{:S(2)}, u32[]{:S(2)}) collective-permute-start(bf16[256,1024]{1,0:T(8,128)(2,1)S(1)} %collective-permute-done.7.refs_7_), channel_id=1, source_target_pairs={{0,8},{8,0},{1,9},{9,1},{2,10},{10,2},{3,11},{11,3},{4,12},{12,4},... | collective-permute-start | bytes 1572872 | tf_op jit(solution)/shard_map/ppermute | solution.py:20
  60.1 7.3 %collective-permute-start.20 = (bf16[256,1024]{1,0:T(8,128)(2,1)S(1)}, bf16[256,1024]{1,0:T(8,128)(2,1)S(1)}, u32[]{:S(2)}, u32[]{:S(2)}) collective-permute-start(bf16[256,1024]{1,0:T(8,128)(2,1)S(1)} %collective-permute-done.9.refs_8_), channel_id=1, source_target_pairs={{0,8},{8,0},{1,9},{9,1},{2,10},{10,2},{3,11},{11,3},{4,12},{12,4},... | collective-permute-start | bytes 1572872 | tf_op jit(solution)/shard_map/ppermute | solution.py:20
  66.0 2.3 %collective-permute-start.19 = (bf16[256,1024]{1,0:T(8,128)(2,1)S(1)}, bf16[256,1024]{1,0:T(8,128)(2,1)S(1)}, u32[]{:S(2)}, u32[]{:S(2)}) collective-permute-start(bf16[256,1024]{1,0:T(8,128)(2,1)S(1)} %collective-permute-done.15.refs_8_), channel_id=1, source_target_pairs={{0,8},{8,0},{1,9},{9,1},{2,10},{10,2},{3,11},{11,3},{4,12},{12,4},... | collective-permute-start | bytes 1572872 | tf_op jit(solution)/shard_map/ppermute | solution.py:20
  66.7 4.3 %collective-permute-start.21 = (bf16[256,1024]{1,0:T(8,128)(2,1)S(1)}, bf16[256,1024]{1,0:T(8,128)(2,1)S(1)}, u32[]{:S(2)}, u32[]{:S(2)}) collective-permute-start(bf16[256,1024]{1,0:T(8,128)(2,1)S(1)} %collective-permute-done.10.refs_9_), channel_id=1, source_target_pairs={{0,8},{8,0},{1,9},{9,1},{2,10},{10,2},{3,11},{11,3},{4,12},{12,4},... | collective-permute-start | bytes 1572872 | tf_op jit(solution)/shard_map/ppermute | solution.py:20
  66.7 4.3 %collective-permute-start.22 = (bf16[256,1024]{1,0:T(8,128)(2,1)S(1)}, bf16[256,1024]{1,0:T(8,128)(2,1)S(1)}, u32[]{:S(2)}, u32[]{:S(2)}) collective-permute-start(bf16[256,1024]{1,0:T(8,128)(2,1)S(1)} %collective-permute-done.11.refs_10_), channel_id=1, source_target_pairs={{0,8},{8,0},{1,9},{9,1},{2,10},{10,2},{3,11},{11,3},{4,12},{12,4},... | collective-permute-start | bytes 1572872 | tf_op jit(solution)/shard_map/ppermute | solution.py:20
  67.3 3.8 %collective-permute-start.23 = (bf16[256,1024]{1,0:T(8,128)(2,1)S(1)}, bf16[256,1024]{1,0:T(8,128)(2,1)S(1)}, u32[]{:S(2)}, u32[]{:S(2)}) collective-permute-start(bf16[256,1024]{1,0:T(8,128)(2,1)S(1)} %collective-permute-done.16.refs_9_), channel_id=1, source_target_pairs={{0,8},{8,0},{1,9},{9,1},{2,10},{10,2},{3,11},{11,3},{4,12},{12,4},... | collective-permute-start | bytes 1572872 | tf_op jit(solution)/shard_map/ppermute | solution.py:20
  67.4 10.3 %collective-permute-start.25 = (bf16[160,1024]{1,0:T(8,128)(2,1)S(1)}, bf16[160,1024]{1,0:T(8,128)(2,1)S(1)}, u32[]{:S(2)}, u32[]{:S(2)}) collective-permute-start(bf16[160,1024]{1,0:T(8,128)(2,1)S(1)} %slice.17), channel_id=1, source_target_pairs={{0,32},{32,64},{64,96},{96,128},{128,160},{160,192},{192,224},{224... | collective-permute-start | bytes 983048 | tf_op jit(solution)/shard_map/ppermute | solution.py:20
  68.3 7.8 %collective-permute-start.24 = (bf16[96,1024]{1,0:T(8,128)(2,1)S(1)}, bf16[96,1024]{1,0:T(8,128)(2,1)S(1)}, u32[]{:S(2)}, u32[]{:S(2)}) collective-permute-start(bf16[96,1024]{1,0:T(8,128)(2,1)S(1)} %slice.16), channel_id=1, source_target_pairs={{0,224},{32,0},{64,32},{96,64},{128,96},{160,128},{192,160},{224,1... | collective-permute-start | bytes 589832 | tf_op jit(solution)/shard_map/ppermute | solution.py:20
